TPU v7x, 32 devices: a whole 2x2x4 slice. The times are simulated.
32 devices in a mesh: section: 2 (over y), ep: 16 (over z, x, core).
Axes of the slice: x: 2, y: 2, z: 4, core: 2. Of those that a mesh axis runs over, the one named last changes fastest.
Arguments:
- grad_output: bfloat16 [2, 2048, 3584], P('section', 'ep'), may hold values from -6 to 6
- route_ids: int32 [2, 2048, 2], P('section', 'ep'), may hold values from 0 to 3, all different within a row; in each aligned block of 128 rows (0 to 127, 128 to 255, ..., all dimensions but the last counted through in order) at most 80 rows name the same one
- route_gates: float32 [2, 2048, 2], P('section', 'ep'), may hold values from 0.25 to 1
- gate_pre: bfloat16 [2, 16, 16, 80, 256], P('section', 'ep'), may hold values from -6 to 6
- up_pre: bfloat16 [2, 16, 16, 80, 256], P('section', 'ep'), may hold values from -6 to 6
- w_gate: bfloat16 [2, 16, 3584, 256], P('section', 'ep'), may hold values from -0.09375 to 0.09375
- w_up: bfloat16 [2, 16, 3584, 256], P('section', 'ep'), may hold values from -0.09375 to 0.09375
- w_down: bfloat16 [2, 16, 256, 3584], P('section', 'ep'), may hold values from -0.1875 to 0.1875
Outputs:
- input_grad: bfloat16 [2, 2048, 3584], P('section', 'ep')
Inputs may be any that keep to these rules, and one draw needn't show every extreme that they name: `route_ids`: in each section the 128 tokens of one index of ep name any expert at most 80 times, a bound that some block reaches; a token names 2 different experts.
All inputs are finite; a program needn't handle non-finite values.
Results may differ from a plain program's by a relative error of at most 0.0072.
Values may be sent and summed in bfloat16 or wider, within the bound.
No kernel may reach another device: no remote copies, remote signals or barrier semaphores. Data moves between devices by JAX's collectives and lax.ppermute only.
A program may use at most 128 MiB of HBM per device.

v0:
```python
import jax
import jax.numpy as jnp
from jax import lax
from jax.sharding import PartitionSpec as P

SPLIT = 4


def shifted(value, axis, steps):
    count = lax.axis_size(axis)
    pairs = [(source, (source + steps) % count) for source in range(count)]
    return lax.ppermute(value, axis, pairs)


def slot_numbers(expert_list, expert_count):
    onehot = (expert_list[:, None] == jnp.arange(expert_count, dtype=jnp.int32)[None, :]).astype(
        jnp.int32
    )
    ranks = jnp.cumsum(onehot, axis=0) - 1
    return jnp.sum(onehot * ranks, axis=1)


def piece_grad(routed_rows, gate_saved, up_saved, gate_matrix, up_matrix, down_matrix):
    contract = (((1,), (1,)), ((), ()))
    hidden_grad = lax.dot_general(
        routed_rows, down_matrix, contract, preferred_element_type=jnp.float32
    )
    gate_value = gate_saved.astype(jnp.float32)
    up_value = up_saved.astype(jnp.float32)
    sigma = jax.nn.sigmoid(gate_value)
    gate_grad = (hidden_grad * up_value * sigma * (1.0 + gate_value * (1.0 - sigma))).astype(
        jnp.bfloat16
    )
    up_grad = (hidden_grad * gate_value * sigma).astype(jnp.bfloat16)
    partial_sum = lax.dot_general(
        gate_grad, gate_matrix, contract, preferred_element_type=jnp.float32
    )
    partial_sum = partial_sum + lax.dot_general(
        up_grad, up_matrix, contract, preferred_element_type=jnp.float32
    )
    return partial_sum.astype(jnp.bfloat16)


def local(grad_output, route_ids, route_gates, gate_pre, up_pre, w_gate, w_up, w_down):
    ep_count = lax.axis_size("ep")
    expert_count = ep_count // SPLIT
    grad_rows = grad_output[0]
    token_count = route_gates.shape[1]
    route_count = route_gates.shape[2]
    model_width = grad_rows.shape[1]
    capacity = gate_pre.shape[3]
    expert_list = route_ids[0].reshape(token_count * route_count)
    slots = slot_numbers(expert_list, expert_count)
    target = expert_list * capacity + slots
    payload = (route_gates[0][:, :, None] * grad_rows[:, None, :].astype(jnp.float32)).astype(
        jnp.bfloat16
    )
    payload = payload.reshape(token_count * route_count, model_width)
    routed = jnp.zeros((expert_count * capacity, model_width), jnp.bfloat16).at[target].set(payload)
    gate_saved = gate_pre[0, 0].reshape(ep_count * capacity, gate_pre.shape[4])
    up_saved = up_pre[0, 0].reshape(ep_count * capacity, up_pre.shape[4])
    outgoing = jnp.broadcast_to(
        routed.reshape(expert_count, 1, capacity, model_width),
        (expert_count, SPLIT, capacity, model_width),
    )
    outgoing = outgoing.reshape(ep_count, capacity, model_width)
    arrived = lax.all_to_all(outgoing, "ep", split_axis=0, concat_axis=0, tiled=True)
    partial_rows = piece_grad(
        arrived.reshape(ep_count * capacity, model_width),
        gate_saved,
        up_saved,
        w_gate[0, 0],
        w_up[0, 0],
        w_down[0, 0],
    )
    returned = lax.all_to_all(
        partial_rows.reshape(ep_count, capacity, model_width),
        "ep",
        split_axis=0,
        concat_axis=0,
        tiled=True,
    )
    combined = jnp.sum(
        returned.reshape(expert_count, SPLIT, capacity, model_width).astype(jnp.float32), axis=1
    ).astype(jnp.bfloat16)
    picked = combined.reshape(expert_count * capacity, model_width)[target].astype(jnp.float32)
    token_grad = jnp.sum(picked.reshape(token_count, route_count, model_width), axis=1).astype(
        jnp.bfloat16
    )
    passed = shifted(token_grad, "section", -1)
    return passed[None]


def solution(mesh):
    placed = (
        P("section", "ep", None),
        P("section", "ep", None),
        P("section", "ep", None),
        P("section", "ep", None, None, None),
        P("section", "ep", None, None, None),
        P("section", "ep", None, None),
        P("section", "ep", None, None),
        P("section", "ep", None, None),
    )
    return jax.shard_map(
        local, mesh=mesh, in_specs=placed, out_specs=P("section", "ep", None), check_vma=False
    )
```

profile of v0, /device:TPU:16, one launch (start us, length us, event | category | flops | bytes accessed | tf_op | source)
XLA Modules:
  0.0 503.6 jit_solution(18333045818895935303)
XLA Ops:
  0.0 0.0 copy-start
  0.0 0.9 copy.12
  0.9 0.1 eq.29
  1.1 0.1 eq.25
  1.2 0.7 broadcast_multiply_fusion
  1.9 1.2 reduce-window.6
  3.1 0.1 slice.10
  3.2 0.1 copy.14
  3.3 0.1 copy.15
  3.4 0.1 add_bitcast_fusion
  3.5 0.1 copy.11
  3.6 0.1 mul.57
  3.8 1.4 bitcast_convert_fusion
  5.1 3.1 mul.61
  8.2 0.0 copy-start.4
  8.2 5.6 %mul.62 = f32[256,3584]{1,0:T(8,128)} reshape(f32[128,2,3584]{2,1,0:T(2,128)} %mul.61) | data formatting | bytes 7340032 | tf_op jit(solution)/shard_map/mul | solution.py:55
  13.9 0.0 copy-done.4
  13.9 0.1 copy.16
  14.0 0.1 mul.59
  14.1 6.3 %scatter_custom_fusion = bf16[320,3584]{1,0:T(8,128)(2,1)} fusion(s32[256]{0:T(256)S(1)} %bitcast.51, f32[256,3584]{1,0:T(8,128)} %mul.62, f32[256]{0:T(256)S(1)} %mul.59, bf16[]{:T(256)} %constant.6.clone.1), kind=kCustom, calls=%fused_computation.9 | custom fusion | flops 1835008 | bytes 5964802 | tf_op jit(solution)/shard_map/scatter | solution.py:59
  20.5 6.0 %broadcast_in_dim.18 = bf16[4,4,80,3584]{3,2,1,0:T(8,128)(2,1)} broadcast(bf16[4,80,3584]{2,1,0:T(8,128)(2,1)} %bitcast.46), dimensions={0,2,3} | broadcast | bytes 11468800 | tf_op jit(solution)/shard_map/broadcast_in_dim | solution.py:62
  26.5 0.0 copy-start.5
  26.5 205.9 %all_to_all.10 = bf16[16,80,3584]{2,1,0:T(8,128)(2,1)S(1)} all-to-all(bf16[16,80,3584]{2,1,0:T(8,128)(2,1)} %bitcast.44), channel_id=1, replica_groups=mesh['section'=2,'ep'=16] {'ep'}, dimensions={0} | all-to-all | bytes 18350080 | tf_op jit(solution)/shard_map/all_to_all | solution.py:67
  232.4 0.0 copy-done.5
  232.4 0.0 copy-start.2
  232.4 0.0 copy-start.3
  232.4 2.6 fusion.5
  235.0 0.0 copy-done
  235.0 0.0 copy-done.2
  235.0 0.0 copy-done.3
  235.0 9.1 %fusion.3 = f32[1280,3584]{1,0:T(8,128)} fusion(bf16[1,1,3584,256]{3,2,1,0:T(8,128)(2,1)S(1)} %copy-done, bf16[1280,256]{1,0:T(8,128)(2,1)S(1)} %bitcast.48, f32[1280,256]{1,0:T(8,128)S(1)} %fusion.5, bf16[1280,256]{1,0:T(8,128)(2,1)S(1)} %bitcast.50), kind=kOutput, calls=%fused_computation.11 | convolution fusion | flops 2352742400 | bytes 22806528 | tf_op jit(solution)/shard_map/dot_general | solution.py:35
  244.2 13.2 %fusion = bf16[1280,3584]{1,0:T(8,128)(2,1)} fusion(f32[1280,3584]{1,0:T(8,128)} %fusion.3, bf16[1,1,3584,256]{3,2,1,0:T(8,128)(2,1)} %param.14, f32[1280,256]{1,0:T(8,128)S(1)} %fusion.5, bf16[1280,256]{1,0:T(8,128)(2,1)} %bitcast.47), kind=kOutput, calls=%fused_computation.3 | convolution fusion | flops 2360279040 | bytes 31326208 | tf_op jit(solution)/shard_map/dot_general | solution.py:38
  257.4 5.1 %all-to-all-start.1 = ((bf16[16,80,3584]{2,1,0:T(8,128)(2,1)}), bf16[16,80,3584]{2,1,0:T(8,128)(2,1)}, u32[]{:S(2)}, u32[]{:S(2)}) async-start(bf16[16,80,3584]{2,1,0:T(8,128)(2,1)} %bitcast.43), calls=%async_computation.1 | async-start | bytes 18350080 | tf_op jit(solution)/shard_map/all_to_all | solution.py:76
  262.5 199.4 %all-to-all-done.1 = bf16[16,80,3584]{2,1,0:T(8,128)(2,1)} async-done(((bf16[16,80,3584]{2,1,0:T(8,128)(2,1)}), bf16[16,80,3584]{2,1,0:T(8,128)(2,1)}, u32[]{:S(2)}, u32[]{:S(2)}) %all-to-all-start.1) | async-done | bytes 9175072 | tf_op jit(solution)/shard_map/all_to_all | solution.py:76
  461.9 5.0 bitcast_reduce_fusion
  466.9 3.0 gather_fusion
  469.9 0.0 copy-start.1
  469.9 4.9 gather.6
  474.8 6.0 %reduce_sum.38 = bf16[128,3584]{1,0:T(8,128)(2,1)S(1)} reduce(bf16[128,2,3584]{2,1,0:T(2,128)(2,1)} %gather.6, bf16[]{:T(256)} %constant.6.clone.1), dimensions={1}, to_apply=%region_5.6 | reduce | flops 458752 | bytes 2752514 | tf_op jit(solution)/shard_map/reduce_sum | solution.py:87
  480.7 1.6 collective-permute-start
  482.3 20.4 %collective-permute-done = bf16[128,3584]{1,0:T(8,128)(2,1)S(1)} collective-permute-done((bf16[128,3584]{1,0:T(8,128)(2,1)S(1)}, bf16[128,3584]{1,0:T(8,128)(2,1)S(1)}, u32[]{:S(2)}, u32[]{:S(2)}) %collective-permute-start) | collective-permute-done | bytes 917536 | tf_op jit(solution)/shard_map/ppermute | solution.py:12
  502.7 0.9 copy.20
  503.6 0.0 copy-done.1
  (6 shorter events, 0.1 us)
Async XLA Ops:
  0.0 235.0 %copy-start = (bf16[1,1,3584,256]{3,2,1,0:T(8,128)(2,1)S(1)}, bf16[1,1,3584,256]{3,2,1,0:T(8,128)(2,1)}, u32[]{:S(2)}) copy-start(bf16[1,1,3584,256]{3,2,1,0:T(8,128)(2,1)} %param.13) | copy-start | bytes 5505028
  8.2 5.7 %copy-start.4 = (f32[1,128,2]{1,2,0:T(2,128)S(1)}, f32[1,128,2]{1,2,0:T(2,128)}, u32[]{:S(2)}) copy-start(f32[1,128,2]{1,2,0:T(2,128)} %param.10) | copy-start | bytes 3076
  26.5 205.9 %copy-start.5 = (bf16[1,1,256,3584]{3,2,1,0:T(8,128)(2,1)S(1)}, bf16[1,1,256,3584]{3,2,1,0:T(8,128)(2,1)}, u32[]{:S(2)}) copy-start(bf16[1,1,256,3584]{3,2,1,0:T(8,128)(2,1)} %param.15) | copy-start | bytes 5505028
  232.4 2.6 copy-start.2
  232.4 2.6 copy-start.3
  257.4 204.6 %all-to-all-start.1 = ((bf16[16,80,3584]{2,1,0:T(8,128)(2,1)}), bf16[16,80,3584]{2,1,0:T(8,128)(2,1)}, u32[]{:S(2)}, u32[]{:S(2)}) async-start(bf16[16,80,3584]{2,1,0:T(8,128)(2,1)} %bitcast.43), calls=%async_computation.1 | async-start | bytes 18350080 | tf_op jit(solution)/shard_map/all_to_all | solution.py:76
  469.9 33.7 %copy-start.1 = (bf16[1,1,3584,256]{3,2,1,0:T(8,128)(2,1)S(1)}, bf16[1,1,3584,256]{3,2,1,0:T(8,128)(2,1)}, u32[]{:S(2)}) copy-start(bf16[1,1,3584,256]{3,2,1,0:T(8,128)(2,1)} %param.13) | copy-start | bytes 5505028
  480.7 22.0 %collective-permute-start = (bf16[128,3584]{1,0:T(8,128)(2,1)S(1)}, bf16[128,3584]{1,0:T(8,128)(2,1)S(1)}, u32[]{:S(2)}, u32[]{:S(2)}) collective-permute-start(bf16[128,3584]{1,0:T(8,128)(2,1)S(1)} %reduce_sum.38), channel_id=1, source_target_pairs={{0,16},{16,0},{1,17},{17,1},{2,18},{18,2},{3,19},{19,3},{4,20},{20... | collective-permute-start | bytes 2752520 | tf_op jit(solution)/shard_map/ppermute | solution.py:12
where the time goes:
time: 505 us; the launch traced here: 504 us
  waiting for transfers between devices  220 us (44%)
  blocking collectives  206 us (41%)
  local copies, waits for them, and re-layouts  25.6 us (5%)
  matrix products  24.9 us (5%)
  other arithmetic  20.6 us (4%)
  starting transfers between devices  6.7 us (1%)
    all_to_all x1, blocking collectives, local(): lax.all_to_all(outgoing, 'ep', split_axis=0, concat_axis=0, tiled=True)  206 us
    all_to_all x1, waiting for transfers between devices, local(): lax.all_to_all(partial_rows.reshape(ep_count, capacity, model_width), 'ep...  199 us
    ppermute x1, waiting for transfers between devices, shifted(): return lax.ppermute(value, axis, pairs)  20.4 us
    dot_general x1, matrix products, piece_grad(): lax.dot_general(up_grad, up_matrix, contract, preferred_element_type=jnp....  13.2 us
  transfers between devices with their start and end apart: 2, of which 2 were waited for; matrix products, arithmetic and copies ran while one was open for 0% of the time, Pallas kernels for 0%

commit v1 on v0

v1 whole, which is shorter than its diff:
```python
import functools

import jax
import jax.numpy as jnp
from jax import lax
from jax.experimental import pallas as pl
from jax.experimental.pallas import tpu as pltpu
from jax.sharding import PartitionSpec as P

SPLIT = 4
MIB = 1 << 20


def exchange(value, mask):
    count = lax.axis_size("ep")
    return lax.ppermute(value, "ep", [(i, i ^ mask) for i in range(count)])


def to_section_before(value, mask):
    sections, count = lax.axis_size("section"), lax.axis_size("ep")
    pairs = [
        (s * count + i, (s - 1) % sections * count + (i ^ mask))
        for s in range(sections)
        for i in range(count)
    ]
    return lax.ppermute(value, ("section", "ep"), pairs)


def column_tile(width):
    for parts in (4, 2):
        if width % (128 * parts) == 0:
            return width // parts
    return width


def fill_choices(own_ref, ids_ref, choice_ref, cap, experts):
    top, tokens = ids_ref.shape
    expert = lax.broadcasted_iota(jnp.int32, (experts, tokens), 0) ^ own_ref[0]
    named = ids_ref[0:1, :] == expert
    for k in range(1, top):
        named = named | (ids_ref[k : k + 1, :] == expert)
    member = jnp.where(named, 1.0, 0.0)
    earlier = lax.broadcasted_iota(jnp.int32, (tokens, tokens), 0) < lax.broadcasted_iota(
        jnp.int32, (tokens, tokens), 1
    )
    slots = jnp.dot(
        member.astype(jnp.bfloat16),
        jnp.where(earlier, 1.0, 0.0).astype(jnp.bfloat16),
        preferred_element_type=jnp.float32,
    )
    slots = jnp.where(named, slots, -1.0)
    place = lax.broadcasted_iota(jnp.int32, (cap, tokens), 0).astype(jnp.float32)
    for k in range(experts):
        choice_ref[k * cap : (k + 1) * cap, :] = jnp.where(
            place == slots[k : k + 1, :], 1.0, 0.0
        ).astype(choice_ref.dtype)


def dispatch_kernel(cap, experts, own_ref, ids_ref, gates_ref, rows_ref, *refs):
    outs, (choice_ref, weight_ref) = refs[:experts], refs[experts:]

    @pl.when(pl.program_id(0) == 0)
    def _():
        fill_choices(own_ref, ids_ref, choice_ref, cap, experts)
        top, tokens = ids_ref.shape
        for k in range(experts):
            expert = own_ref[0] ^ k
            gate = jnp.zeros((1, tokens), jnp.float32)
            for j in range(top):
                gate = jnp.where(ids_ref[j : j + 1, :] == expert, gates_ref[j : j + 1, :], gate)
            chosen = choice_ref[k * cap : (k + 1) * cap, :].astype(jnp.float32)
            weight_ref[k * cap : (k + 1) * cap, :] = jnp.sum(chosen * gate, axis=1, keepdims=True)

    picked = jnp.dot(choice_ref[...], rows_ref[...], preferred_element_type=jnp.float32)
    payload = (picked * weight_ref[...]).astype(jnp.bfloat16)
    for k in range(experts):
        outs[k][...] = payload[k * cap : (k + 1) * cap, :]


def dispatch(own, ids, gates, rows, cap, experts):
    tokens, width = rows.shape
    tile = column_tile(width)
    whole = pl.BlockSpec(ids.shape, lambda i, own: (0, 0))
    return pl.pallas_call(
        functools.partial(dispatch_kernel, cap, experts),
        grid_spec=pltpu.PrefetchScalarGridSpec(
            num_scalar_prefetch=1,
            grid=(width // tile,),
            in_specs=[whole, whole, pl.BlockSpec((tokens, tile), lambda i, own: (0, i))],
            out_specs=[pl.BlockSpec((cap, tile), lambda i, own: (0, i))] * experts,
            scratch_shapes=[
                pltpu.VMEM((experts * cap, tokens), jnp.bfloat16),
                pltpu.VMEM((experts * cap, 1), jnp.float32),
            ],
        ),
        out_shape=[jax.ShapeDtypeStruct((cap, width), jnp.bfloat16)] * experts,
        compiler_params=pltpu.CompilerParams(vmem_limit_bytes=16 * MIB),
        cost_estimate=pl.CostEstimate(
            flops=2 * experts * cap * tokens * width, bytes_accessed=4 * MIB, transcendentals=0
        ),
        name="dispatch",
    )(own, ids, gates, rows)


def combine_kernel(cap, experts, own_ref, ids_ref, *refs):
    rows, out_ref, choice_ref = refs[:experts], refs[experts], refs[experts + 1]

    @pl.when(pl.program_id(0) == 0)
    def _():
        fill_choices(own_ref, ids_ref, choice_ref, cap, experts)

    total = None
    for k in range(experts):
        part = lax.dot_general(
            choice_ref[k * cap : (k + 1) * cap, :],
            rows[k][...],
            (((0,), (0,)), ((), ())),
            preferred_element_type=jnp.float32,
        )
        total = part if total is None else total + part
    out_ref[...] = total.astype(jnp.bfloat16)


def combine(own, ids, returned, cap, experts):
    width, tokens = returned[0].shape[1], ids.shape[1]
    tile = column_tile(width)
    return pl.pallas_call(
        functools.partial(combine_kernel, cap, experts),
        grid_spec=pltpu.PrefetchScalarGridSpec(
            num_scalar_prefetch=1,
            grid=(width // tile,),
            in_specs=[pl.BlockSpec(ids.shape, lambda i, own: (0, 0))]
            + [pl.BlockSpec((cap, tile), lambda i, own: (0, i))] * experts,
            out_specs=pl.BlockSpec((tokens, tile), lambda i, own: (0, i)),
            scratch_shapes=[pltpu.VMEM((experts * cap, tokens), jnp.bfloat16)],
        ),
        out_shape=jax.ShapeDtypeStruct((tokens, width), jnp.bfloat16),
        compiler_params=pltpu.CompilerParams(vmem_limit_bytes=16 * MIB),
        cost_estimate=pl.CostEstimate(
            flops=2 * experts * cap * tokens * width, bytes_accessed=4 * MIB, transcendentals=0
        ),
        name="combine",
    )(own, ids, *returned)


def pieces_kernel(parts, source_ref, *refs):
    blocks = refs[:SPLIT]
    gate_ref, up_ref, w_gate_ref, w_up_ref, w_down_ref = refs[SPLIT : SPLIT + 5]
    outs = refs[SPLIT + 5 : 2 * SPLIT + 5]
    rows, gates, ups, w_gate, w_up, w_down, result, row_sem, act_sem, down_sem, up_sem, out_sem = refs[
        2 * SPLIT + 5 :
    ]
    cap, width = blocks[0].shape
    hidden = w_down.shape[0]
    tile = width // parts

    def columns(i):
        return pl.ds(i * tile, tile)

    row_copies, down_copies, act_copies, weight_copies = [], [], [], []
    for i in range(parts):
        down_copies.append(
            pltpu.make_async_copy(
                w_down_ref.at[:, columns(i)], w_down.at[:, columns(i)], down_sem.at[i]
            )
        )
        for j in range(SPLIT):
            row_copies.append(
                pltpu.make_async_copy(
                    blocks[j].at[:, columns(i)],
                    rows.at[pl.ds(j * cap, cap), columns(i)],
                    row_sem.at[i, j],
                )
            )
    for j in range(SPLIT):
        at = pl.ds(j * cap, cap)
        act_copies.append(
            pltpu.make_async_copy(gate_ref.at[source_ref[j]], gates.at[at], act_sem.at[0, j])
        )
        act_copies.append(
            pltpu.make_async_copy(up_ref.at[source_ref[j]], ups.at[at], act_sem.at[1, j])
        )
    for i in range(parts):
        weight_copies.append(
            pltpu.make_async_copy(w_gate_ref.at[columns(i)], w_gate.at[columns(i)], up_sem.at[0, i])
        )
        weight_copies.append(
            pltpu.make_async_copy(w_up_ref.at[columns(i)], w_up.at[columns(i)], up_sem.at[1, i])
        )
    for copy in [*row_copies, *down_copies, *act_copies, *weight_copies]:
        copy.start()
    across = (((1,), (1,)), ((), ()))
    total = jnp.zeros((SPLIT * cap, hidden), jnp.float32)
    for i in range(parts):
        down_copies[i].wait()
        for j in range(SPLIT):
            row_copies[i * SPLIT + j].wait()
        total = total + lax.dot_general(
            rows[:, columns(i)], w_down[:, columns(i)], across, preferred_element_type=jnp.float32
        )
    for copy in act_copies:
        copy.wait()
    g = gates[...].astype(jnp.float32)
    u = ups[...].astype(jnp.float32)
    s = jax.nn.sigmoid(g)
    gate_grad = (total * u * s * (1.0 + g * (1.0 - s))).astype(jnp.bfloat16)
    up_grad = (total * g * s).astype(jnp.bfloat16)
    out_copies = []
    for i in range(parts):
        weight_copies[2 * i].wait()
        weight_copies[2 * i + 1].wait()
        part = lax.dot_general(
            gate_grad, w_gate[columns(i), :], across, preferred_element_type=jnp.float32
        )
        part = part + lax.dot_general(
            up_grad, w_up[columns(i), :], across, preferred_element_type=jnp.float32
        )
        result[:, columns(i)] = part.astype(jnp.bfloat16)
        for j in range(SPLIT):
            copy = pltpu.make_async_copy(
                result.at[pl.ds(j * cap, cap), columns(i)],
                outs[j].at[:, columns(i)],
                out_sem.at[i, j],
            )
            copy.start()
            out_copies.append(copy)
    for copy in out_copies:
        copy.wait()


def pieces(source, blocks, gate_pre, up_pre, w_gate, w_up, w_down):
    cap, width = blocks[0].shape
    hidden = w_down.shape[0]
    parts = width // column_tile(width)
    anywhere = pl.BlockSpec(memory_space=pl.ANY)
    rows = SPLIT * cap
    return pl.pallas_call(
        functools.partial(pieces_kernel, parts),
        in_specs=[pl.BlockSpec(memory_space=pltpu.SMEM)] + [anywhere] * (SPLIT + 5),
        out_specs=[anywhere] * SPLIT,
        out_shape=[jax.ShapeDtypeStruct((cap, width), jnp.bfloat16)] * SPLIT,
        scratch_shapes=[
            pltpu.VMEM((rows, width), jnp.bfloat16),
            pltpu.VMEM((rows, hidden), jnp.bfloat16),
            pltpu.VMEM((rows, hidden), jnp.bfloat16),
            pltpu.VMEM((width, hidden), jnp.bfloat16),
            pltpu.VMEM((width, hidden), jnp.bfloat16),
            pltpu.VMEM((hidden, width), jnp.bfloat16),
            pltpu.VMEM((rows, width), jnp.bfloat16),
            pltpu.SemaphoreType.DMA((parts, SPLIT)),
            pltpu.SemaphoreType.DMA((2, SPLIT)),
            pltpu.SemaphoreType.DMA((parts,)),
            pltpu.SemaphoreType.DMA((2, parts)),
            pltpu.SemaphoreType.DMA((parts, SPLIT)),
        ],
        compiler_params=pltpu.CompilerParams(vmem_limit_bytes=24 * MIB),
        cost_estimate=pl.CostEstimate(
            flops=6 * rows * width * hidden, bytes_accessed=12 * MIB, transcendentals=rows * hidden
        ),
        name="pieces",
    )(source, *blocks, gate_pre, up_pre, w_gate, w_up, w_down)


def added(a, b):
    return (a.astype(jnp.float32) + b.astype(jnp.float32)).astype(jnp.bfloat16)


def local(grad_output, route_ids, route_gates, gate_pre, up_pre, w_gate, w_up, w_down):
    experts = lax.axis_size("ep") // SPLIT
    me = lax.axis_index("ep")
    own, seat = me // SPLIT, me % SPLIT
    cap = gate_pre.shape[3]
    gate_saved, up_saved = gate_pre[0, 0], up_pre[0, 0]
    spare = -cap % 16
    if spare:
        gate_saved = jnp.pad(gate_saved, ((0, 0), (0, spare), (0, 0)))
        up_saved = jnp.pad(up_saved, ((0, 0), (0, spare), (0, 0)))
        cap += spare
    ids = route_ids[0].T
    own = own.astype(jnp.int32).reshape(1)
    ids_after = to_section_before(ids, 0)
    outgoing = dispatch(own, ids, route_gates[0].T, grad_output[0], cap, experts)
    returned = []
    for k in range(experts):
        mine = exchange(outgoing[k], k * SPLIT) if k else outgoing[k]
        far = exchange(mine, 2)
        blocks = [mine, exchange(mine, 1), far, exchange(far, 1)]
        source = ((own ^ k) * SPLIT + (seat ^ jnp.arange(SPLIT, dtype=jnp.int32))).astype(jnp.int32)
        partial = pieces(source, blocks, gate_saved, up_saved, w_gate[0, 0], w_up[0, 0], w_down[0, 0])
        near_sum = added(partial[0], exchange(partial[1], 1))
        far_sum = added(partial[2], exchange(partial[3], 1))
        whole_sum = added(near_sum, exchange(far_sum, 2))
        returned.append(to_section_before(whole_sum, k * SPLIT))
    return combine(own, ids_after, returned, cap, experts)[None]


def solution(mesh):
    placed = (
        P("section", "ep", None),
        P("section", "ep", None),
        P("section", "ep", None),
        P("section", "ep", None, None, None),
        P("section", "ep", None, None, None),
        P("section", "ep", None, None),
        P("section", "ep", None, None),
        P("section", "ep", None, None),
    )
    return jax.shard_map(
        local, mesh=mesh, in_specs=placed, out_specs=P("section", "ep", None), check_vma=False
    )
```

time: 505 us -> 199 us (0.39)
  the two profiles are of different devices: /device:TPU:16 before, /device:TPU:0 now
where the time goes in v1:
time: 199 us
  waiting for transfers between devices  122 us (61%)
  Pallas kernels  42.9 us (22%)
  starting transfers between devices  24.2 us (12%)
  local copies, waits for them, and re-layouts  8.21 us (4%)
    ppermute x27, waiting for transfers between devices, exchange(): return lax.ppermute(value, 'ep', [(i, i ^ mask) for i in range(count)])  88.2 us
    pallas_call x4, Pallas kernels, pieces(): pl.pallas_call(functools.partial(pieces_kernel, parts), in_specs=[pl.Bloc...  37 us
    ppermute x5, waiting for transfers between devices, to_section_before(): return lax.ppermute(value, ('section', 'ep'), pairs)  33.8 us
    ppermute x27, starting transfers between devices, exchange(): return lax.ppermute(value, 'ep', [(i, i ^ mask) for i in range(count)])  17.5 us
    unnamed x24, local copies, waits for them, and re-layouts  8.21 us
    ppermute x5, starting transfers between devices, to_section_before(): return lax.ppermute(value, ('section', 'ep'), pairs)  6.71 us
  transfers between devices with their start and end apart: 32, of which 9 were waited for; matrix products, arithmetic and copies ran while one was open for 1% of the time, Pallas kernels for 19%

profile of v1, /device:TPU:0, one launch (start us, length us, event | category | flops | bytes accessed | tf_op | source)
XLA Modules:
  0.0 198.7 jit_solution(4253210775201083115)
XLA Ops:
  0.0 1.2 copy-done.8
  1.3 0.7 copy-done.9
  1.9 0.7 copy-done.10
  2.6 2.9 %dispatch.1 = (bf16[80,3584]{1,0:T(8,128)(2,1)S(1)}, bf16[80,3584]{1,0:T(8,128)(2,1)}, bf16[80,3584]{1,0:T(8,128)(2,1)}, bf16[80,3584]{1,0:T(8,128)(2,1)}) custom-call(s32[1]{0:T(128)} %bitcast.own_ref, s32[2,128]{1,0:T(2,128)S(1)} %bitcast.40, f32[2,128]{1,0:T(2,128)S(1)} %bitcast.39, bf16[128,3584]{1,0:T(8,128)(2,1)S(1)} %bitcast.38), custom_call_target="tpu_custom_call" | custom-call | flops 293601280 | bytes 4194304 | tf_op jit(solution)/shard_map/dispatch/pallas_call | solution.py:84
  5.5 2.9 %collective-permute-start.2 = (bf16[80,3584]{1,0:T(8,128)(2,1)S(1)}, bf16[80,3584]{1,0:T(8,128)(2,1)S(1)}, u32[]{:S(2)}, u32[]{:S(2)}) collective-permute-start(bf16[80,3584]{1,0:T(8,128)(2,1)S(1)} %get-tuple-element.25.refs_0_), channel_id=1, source_target_pairs={{0,2},{1,3},{2,0},{3,1},{4,6},{5,7},{6,4},{7,5},{8,10},{9,11},{10,... | collective-permute-start | bytes 1720328 | tf_op jit(solution)/shard_map/ppermute | solution.py:16
  8.4 3.6 %collective-permute-start.24 = (bf16[80,3584]{1,0:T(8,128)(2,1)}, bf16[80,3584]{1,0:T(8,128)(2,1)S(1)}, u32[]{:S(2)}, u32[]{:S(2)}) collective-permute-start(bf16[80,3584]{1,0:T(8,128)(2,1)} %get-tuple-element.40), channel_id=1, source_target_pairs={{0,12},{1,13},{2,14},{3,15},{4,8},{5,9},{6,10},{7,11},{8,4},{9,5},... | collective-permute-start | bytes 1720328 | tf_op jit(solution)/shard_map/ppermute | solution.py:16
  12.0 0.0 collective-permute-start.16
  12.0 0.8 collective-permute-start.8
  12.8 0.0 collective-permute-start.1
  12.8 8.6 %collective-permute-done.2.refs_2_ = bf16[80,3584]{1,0:T(8,128)(2,1)S(1)} collective-permute-done((bf16[80,3584]{1,0:T(8,128)(2,1)S(1)}, bf16[80,3584]{1,0:T(8,128)(2,1)S(1)}, u32[]{:S(2)}, u32[]{:S(2)}) %collective-permute-start.2) | collective-permute-done | bytes 573472 | tf_op jit(solution)/shard_map/ppermute | solution.py:16
  21.4 0.0 collective-permute-start.3
  21.4 5.0 %collective-permute-done.24.refs_0_ = bf16[80,3584]{1,0:T(8,128)(2,1)S(1)} collective-permute-done((bf16[80,3584]{1,0:T(8,128)(2,1)}, bf16[80,3584]{1,0:T(8,128)(2,1)S(1)}, u32[]{:S(2)}, u32[]{:S(2)}) %collective-permute-start.24) | collective-permute-done | bytes 573472 | tf_op jit(solution)/shard_map/ppermute | solution.py:16
  26.4 0.3 collective-permute-start.26
  26.7 34.2 %collective-permute-done.16.refs_0_ = bf16[80,3584]{1,0:T(8,128)(2,1)S(1)} collective-permute-done((bf16[80,3584]{1,0:T(8,128)(2,1)}, bf16[80,3584]{1,0:T(8,128)(2,1)S(1)}, u32[]{:S(2)}, u32[]{:S(2)}) %collective-permute-start.16) | collective-permute-done | bytes 573472 | tf_op jit(solution)/shard_map/ppermute | solution.py:16
  60.9 0.5 collective-permute-start.18
  61.5 0.0 collective-permute-done.1.refs_1_
  61.5 1.5 collective-permute-start.10
  63.0 1.5 copy-done
  64.5 1.5 copy-done.2
  66.0 1.5 copy-done.4
  67.5 1.1 copy-done.7
  68.6 9.1 %pieces.4 = (bf16[80,3584]{1,0:T(8,128)(2,1)S(1)}, bf16[80,3584]{1,0:T(8,128)(2,1)S(1)}, bf16[80,3584]{1,0:T(8,128)(2,1)S(1)}, bf16[80,3584]{1,0:T(8,128)(2,1)S(1)}) custom-call(s32[4]{0:T(128)S(1)} %fusion.3.source_ref, bf16[80,3584]{1,0:T(8,128)(2,1)S(1)} %get-tuple-element.25.refs_0_, bf16[80,3584]{1,0:T(8,128)(2,1)} %collective-permute-done.1.refs_1_, ...), custom_call_target="tpu_custom_call" | custom-call | flops 1761607680 | bytes 12582912 | tf_op jit(solution)/shard_map/pieces/pallas_call | solution.py:237
  77.7 0.1 collective-permute-start.5
  77.8 0.0 collective-permute-done.26.refs_2_
  77.8 0.5 collective-permute-start.17
  78.3 0.0 collective-permute-done.25.refs_1_
  78.3 0.1 collective-permute-start.9
  78.4 0.4 collective-permute-start.27
  78.8 9.8 %collective-permute-done.10.refs_2_ = bf16[80,3584]{1,0:T(8,128)(2,1)S(1)} collective-permute-done((bf16[80,3584]{1,0:T(8,128)(2,1)S(1)}, bf16[80,3584]{1,0:T(8,128)(2,1)S(1)}, u32[]{:S(2)}, u32[]{:S(2)}) %collective-permute-start.10) | collective-permute-done | bytes 573472 | tf_op jit(solution)/shard_map/ppermute | solution.py:16
  88.6 0.0 collective-permute-start.19
  88.6 0.5 collective-permute-start.11
  89.1 0.1 add_convert_fusion.10
  89.3 0.1 collective-permute-start.4
  89.4 0.6 collective-permute-start.6
  90.0 9.2 %pieces.7 = (bf16[80,3584]{1,0:T(8,128)(2,1)S(1)}, bf16[80,3584]{1,0:T(8,128)(2,1)S(1)}, bf16[80,3584]{1,0:T(8,128)(2,1)S(1)}, bf16[80,3584]{1,0:T(8,128)(2,1)S(1)}) custom-call(s32[4]{0:T(128)S(1)} %fusion.source_ref, bf16[80,3584]{1,0:T(8,128)(2,1)S(1)} %collective-permute-done.24.refs_0_, bf16[80,3584]{1,0:T(8,128)(2,1)S(1)} %collective-permute-done.25.refs_1_, ...), custom_call_target="tpu_custom_call" | custom-call | flops 1761607680 | bytes 12582912 | tf_op jit(solution)/shard_map/pieces/pallas_call | solution.py:237
  99.3 0.2 collective-permute-start.29
  99.5 9.4 %pieces.6 = (bf16[80,3584]{1,0:T(8,128)(2,1)S(1)}, bf16[80,3584]{1,0:T(8,128)(2,1)S(1)}, bf16[80,3584]{1,0:T(8,128)(2,1)S(1)}, bf16[80,3584]{1,0:T(8,128)(2,1)S(1)}) custom-call(s32[4]{0:T(128)S(1)} %fusion.1.source_ref, bf16[80,3584]{1,0:T(8,128)(2,1)S(1)} %collective-permute-done.16.refs_0_, bf16[80,3584]{1,0:T(8,128)(2,1)S(1)} %collective-permute-done.17.refs_1_, ...), custom_call_target="tpu_custom_call" | custom-call | flops 1761607680 | bytes 12582912 | tf_op jit(solution)/shard_map/pieces/pallas_call | solution.py:237
  108.9 0.4 collective-permute-start.28
  109.3 0.2 collective-permute-start.21
  109.5 9.2 %pieces.5 = (bf16[80,3584]{1,0:T(8,128)(2,1)S(1)}, bf16[80,3584]{1,0:T(8,128)(2,1)S(1)}, bf16[80,3584]{1,0:T(8,128)(2,1)S(1)}, bf16[80,3584]{1,0:T(8,128)(2,1)S(1)}) custom-call(s32[4]{0:T(128)S(1)} %fusion.2.source_ref, bf16[80,3584]{1,0:T(8,128)(2,1)S(1)} %collective-permute-done.8.refs_0_, bf16[80,3584]{1,0:T(8,128)(2,1)S(1)} %collective-permute-done.9.refs_1_, ...), custom_call_target="tpu_custom_call" | custom-call | flops 1761607680 | bytes 12582912 | tf_op jit(solution)/shard_map/pieces/pallas_call | solution.py:237
  118.8 0.4 collective-permute-start.20
  119.2 0.2 collective-permute-start.13
  119.3 0.2 add_convert_fusion.9
  119.6 0.4 collective-permute-start.12
  120.0 0.1 add_convert_fusion.1
  120.1 1.5 collective-permute-start.30
  121.7 0.1 add_convert_fusion.4
  121.8 1.3 collective-permute-start.22
  123.1 0.1 add_convert_fusion.7
  123.3 0.9 collective-permute-start.14
  124.1 11.9 %collective-permute-done.30 = bf16[80,3584]{1,0:T(8,128)(2,1)S(1)} collective-permute-done((bf16[80,3584]{1,0:T(8,128)(2,1)S(1)}, bf16[80,3584]{1,0:T(8,128)(2,1)S(1)}, u32[]{:S(2)}, u32[]{:S(2)}) %collective-permute-start.30) | collective-permute-done | bytes 573472 | tf_op jit(solution)/shard_map/ppermute | solution.py:16
  136.0 1.5 collective-permute-start.7
  137.5 0.2 add_convert_fusion
  137.7 2.5 %collective-permute-start.31 = (bf16[80,3584]{1,0:T(8,128)(2,1)S(1)}, bf16[80,3584]{1,0:T(8,128)(2,1)S(1)}, u32[]{:S(2)}, u32[]{:S(2)}) collective-permute-start(bf16[80,3584]{1,0:T(8,128)(2,1)S(1)} %add_convert_fusion), channel_id=1, source_target_pairs={{0,28},{1,29},{2,30},{3,31},{4,24},{5,25},{6,26},{7,27},{8,20},{9,... | collective-permute-start | bytes 1720328 | tf_op jit(solution)/shard_map/ppermute | solution.py:26
  140.2 8.1 %collective-permute-done.22 = bf16[80,3584]{1,0:T(8,128)(2,1)S(1)} collective-permute-done((bf16[80,3584]{1,0:T(8,128)(2,1)S(1)}, bf16[80,3584]{1,0:T(8,128)(2,1)S(1)}, u32[]{:S(2)}, u32[]{:S(2)}) %collective-permute-start.22) | collective-permute-done | bytes 573472 | tf_op jit(solution)/shard_map/ppermute | solution.py:16
  148.3 0.2 add_convert_fusion.3
  148.5 0.7 collective-permute-start.23
  149.2 10.6 %collective-permute-done.14 = bf16[80,3584]{1,0:T(8,128)(2,1)S(1)} collective-permute-done((bf16[80,3584]{1,0:T(8,128)(2,1)S(1)}, bf16[80,3584]{1,0:T(8,128)(2,1)S(1)}, u32[]{:S(2)}, u32[]{:S(2)}) %collective-permute-start.14) | collective-permute-done | bytes 573472 | tf_op jit(solution)/shard_map/ppermute | solution.py:16
  159.8 0.2 add_convert_fusion.6
  160.0 0.8 collective-permute-start.15
  160.8 1.2 collective-permute-start
  162.0 2.5 %collective-permute-done.ids_ref = s32[2,128]{1,0:T(2,128)S(1)} collective-permute-done((s32[2,128]{1,0:T(2,128)S(1)}, s32[2,128]{1,0:T(2,128)S(1)}, u32[]{:S(2)}, u32[]{:S(2)}) %collective-permute-start) | collective-permute-done | bytes 1056 | tf_op jit(solution)/shard_map/ppermute | solution.py:26
  164.5 31.3 %collective-permute-done.23.refs_2_ = bf16[80,3584]{1,0:T(8,128)(2,1)S(1)} collective-permute-done((bf16[80,3584]{1,0:T(8,128)(2,1)S(1)}, bf16[80,3584]{1,0:T(8,128)(2,1)S(1)}, u32[]{:S(2)}, u32[]{:S(2)}) %collective-permute-start.23) | collective-permute-done | bytes 573472 | tf_op jit(solution)/shard_map/ppermute | solution.py:26
  195.8 3.0 %combine.1 = bf16[128,3584]{1,0:T(8,128)(2,1)} custom-call(s32[1]{0:T(128)} %bitcast.own_ref, s32[2,128]{1,0:T(2,128)S(1)} %collective-permute-done.ids_ref, bf16[80,3584]{1,0:T(8,128)(2,1)S(1)} %collective-permute-done.7.refs_0_, bf16[80,3584]{1,0:T(8,128)(2,1)S(1)} %collective-permute-done.15.refs_1_, ...), custom_call_target="tpu_custom_call" | custom-call | flops 293601280 | bytes 4194304 | tf_op jit(solution)/shard_map/combine/pallas_call | solution.py:127
  (42 shorter events, 0.1 us)
Async XLA Ops:
  0.0 63.0 %copy-start.6 = (bf16[1,1,16,80,256]{4,3,2,1,0:T(8,128)(2,1)S(1)}, bf16[1,1,16,80,256]{4,3,2,1,0:T(8,128)(2,1)}, u32[]{:S(2)}) copy-start(bf16[1,1,16,80,256]{4,3,2,1,0:T(8,128)(2,1)} %param.11) | copy-start | bytes 1966084
  0.0 1.2 copy-start.8
  1.2 0.7 copy-start.9
  1.9 0.7 copy-start.10
  5.5 15.9 %collective-permute-start.2 = (bf16[80,3584]{1,0:T(8,128)(2,1)S(1)}, bf16[80,3584]{1,0:T(8,128)(2,1)S(1)}, u32[]{:S(2)}, u32[]{:S(2)}) collective-permute-start(bf16[80,3584]{1,0:T(8,128)(2,1)S(1)} %get-tuple-element.25.refs_0_), channel_id=1, source_target_pairs={{0,2},{1,3},{2,0},{3,1},{4,6},{5,7},{6,4},{7,5},{8,10},{9,11},{10,... | collective-permute-start | bytes 1720328 | tf_op jit(solution)/shard_map/ppermute | solution.py:16
  8.4 18.0 %collective-permute-start.24 = (bf16[80,3584]{1,0:T(8,128)(2,1)}, bf16[80,3584]{1,0:T(8,128)(2,1)S(1)}, u32[]{:S(2)}, u32[]{:S(2)}) collective-permute-start(bf16[80,3584]{1,0:T(8,128)(2,1)} %get-tuple-element.40), channel_id=1, source_target_pairs={{0,12},{1,13},{2,14},{3,15},{4,8},{5,9},{6,10},{7,11},{8,4},{9,5},... | collective-permute-start | bytes 1720328 | tf_op jit(solution)/shard_map/ppermute | solution.py:16
  12.0 48.9 %collective-permute-start.16 = (bf16[80,3584]{1,0:T(8,128)(2,1)}, bf16[80,3584]{1,0:T(8,128)(2,1)S(1)}, u32[]{:S(2)}, u32[]{:S(2)}) collective-permute-start(bf16[80,3584]{1,0:T(8,128)(2,1)} %get-tuple-element.35), channel_id=1, source_target_pairs={{0,8},{1,9},{2,10},{3,11},{4,12},{5,13},{6,14},{7,15},{8,0},{9,1},... | collective-permute-start | bytes 1720328 | tf_op jit(solution)/shard_map/ppermute | solution.py:16
  12.0 48.9 %collective-permute-start.8 = (bf16[80,3584]{1,0:T(8,128)(2,1)}, bf16[80,3584]{1,0:T(8,128)(2,1)S(1)}, u32[]{:S(2)}, u32[]{:S(2)}) collective-permute-start(bf16[80,3584]{1,0:T(8,128)(2,1)} %get-tuple-element.30), channel_id=1, source_target_pairs={{0,4},{1,5},{2,6},{3,7},{4,0},{5,1},{6,2},{7,3},{8,12},{9,13},{10,... | collective-permute-start | bytes 1720328 | tf_op jit(solution)/shard_map/ppermute | solution.py:16
  12.8 48.7 %collective-permute-start.1 = (bf16[80,3584]{1,0:T(8,128)(2,1)S(1)}, bf16[80,3584]{1,0:T(8,128)(2,1)}, u32[]{:S(2)}, u32[]{:S(2)}) collective-permute-start(bf16[80,3584]{1,0:T(8,128)(2,1)S(1)} %get-tuple-element.25.refs_0_), channel_id=1, source_target_pairs={{0,1},{1,0},{2,3},{3,2},{4,5},{5,4},{6,7},{7,6},{8,9},{9,8},{10,11... | collective-permute-start | bytes 1720328 | tf_op jit(solution)/shard_map/ppermute | solution.py:16
  21.4 41.6 %collective-permute-start.3 = (bf16[80,3584]{1,0:T(8,128)(2,1)S(1)}, bf16[80,3584]{1,0:T(8,128)(2,1)}, u32[]{:S(2)}, u32[]{:S(2)}) collective-permute-start(bf16[80,3584]{1,0:T(8,128)(2,1)S(1)} %collective-permute-done.2.refs_2_), channel_id=1, source_target_pairs={{0,1},{1,0},{2,3},{3,2},{4,5},{5,4},{6,7},{7,6},{8,9},{9,8},{10,11... | collective-permute-start | bytes 1720328 | tf_op jit(solution)/shard_map/ppermute | solution.py:16
  26.4 51.4 %collective-permute-start.26 = (bf16[80,3584]{1,0:T(8,128)(2,1)S(1)}, bf16[80,3584]{1,0:T(8,128)(2,1)S(1)}, u32[]{:S(2)}, u32[]{:S(2)}) collective-permute-start(bf16[80,3584]{1,0:T(8,128)(2,1)S(1)} %collective-permute-done.24.refs_0_), channel_id=1, source_target_pairs={{0,2},{1,3},{2,0},{3,1},{4,6},{5,7},{6,4},{7,5},{8,10},{9,11},{10,... | collective-permute-start | bytes 1720328 | tf_op jit(solution)/shard_map/ppermute | solution.py:16
  60.9 17.4 %collective-permute-start.25 = (bf16[80,3584]{1,0:T(8,128)(2,1)S(1)}, bf16[80,3584]{1,0:T(8,128)(2,1)S(1)}, u32[]{:S(2)}, u32[]{:S(2)}) collective-permute-start(bf16[80,3584]{1,0:T(8,128)(2,1)S(1)} %collective-permute-done.24.refs_0_), channel_id=1, source_target_pairs={{0,1},{1,0},{2,3},{3,2},{4,5},{5,4},{6,7},{7,6},{8,9},{9,8},{10,11... | collective-permute-start | bytes 1720328 | tf_op jit(solution)/shard_map/ppermute | solution.py:16
  60.9 17.5 %collective-permute-start.18 = (bf16[80,3584]{1,0:T(8,128)(2,1)S(1)}, bf16[80,3584]{1,0:T(8,128)(2,1)S(1)}, u32[]{:S(2)}, u32[]{:S(2)}) collective-permute-start(bf16[80,3584]{1,0:T(8,128)(2,1)S(1)} %collective-permute-done.16.refs_0_), channel_id=1, source_target_pairs={{0,2},{1,3},{2,0},{3,1},{4,6},{5,7},{6,4},{7,5},{8,10},{9,11},{10,... | collective-permute-start | bytes 1720328 | tf_op jit(solution)/shard_map/ppermute | solution.py:16
  61.5 27.1 %collective-permute-start.10 = (bf16[80,3584]{1,0:T(8,128)(2,1)S(1)}, bf16[80,3584]{1,0:T(8,128)(2,1)S(1)}, u32[]{:S(2)}, u32[]{:S(2)}) collective-permute-start(bf16[80,3584]{1,0:T(8,128)(2,1)S(1)} %collective-permute-done.8.refs_0_), channel_id=1, source_target_pairs={{0,2},{1,3},{2,0},{3,1},{4,6},{5,7},{6,4},{7,5},{8,10},{9,11},{10,... | collective-permute-start | bytes 1720328 | tf_op jit(solution)/shard_map/ppermute | solution.py:16
  63.0 1.5 copy-start
  64.5 1.5 copy-start.2
  66.0 1.5 copy-start.4
  67.5 1.1 copy-start.7
  68.6 21.4 %copy-start.1 = (bf16[1,1,3584,256]{3,2,1,0:T(8,128)(2,1)S(1)}, bf16[1,1,3584,256]{3,2,1,0:T(8,128)(2,1)}, u32[]{:S(2)}) copy-start(bf16[1,1,3584,256]{3,2,1,0:T(8,128)(2,1)} %param.13) | copy-start | bytes 5505028
  68.6 21.4 %copy-start.3 = (bf16[1,1,3584,256]{3,2,1,0:T(8,128)(2,1)S(1)}, bf16[1,1,3584,256]{3,2,1,0:T(8,128)(2,1)}, u32[]{:S(2)}) copy-start(bf16[1,1,3584,256]{3,2,1,0:T(8,128)(2,1)} %param.14) | copy-start | bytes 5505028
  68.6 21.4 %copy-start.5 = (bf16[1,1,256,3584]{3,2,1,0:T(8,128)(2,1)S(1)}, bf16[1,1,256,3584]{3,2,1,0:T(8,128)(2,1)}, u32[]{:S(2)}) copy-start(bf16[1,1,256,3584]{3,2,1,0:T(8,128)(2,1)} %param.15) | copy-start | bytes 5505028
  77.7 10.9 %collective-permute-start.5 = (bf16[80,3584]{1,0:T(8,128)(2,1)S(1)}, bf16[80,3584]{1,0:T(8,128)(2,1)S(1)}, u32[]{:S(2)}, u32[]{:S(2)}) collective-permute-start(bf16[80,3584]{1,0:T(8,128)(2,1)S(1)} %get-tuple-element.29), channel_id=1, source_target_pairs={{0,1},{1,0},{2,3},{3,2},{4,5},{5,4},{6,7},{7,6},{8,9},{9,8},{10,11... | collective-permute-start | bytes 1720328 | tf_op jit(solution)/shard_map/ppermute | solution.py:16
  77.8 11.5 %collective-permute-start.17 = (bf16[80,3584]{1,0:T(8,128)(2,1)S(1)}, bf16[80,3584]{1,0:T(8,128)(2,1)S(1)}, u32[]{:S(2)}, u32[]{:S(2)}) collective-permute-start(bf16[80,3584]{1,0:T(8,128)(2,1)S(1)} %collective-permute-done.16.refs_0_), channel_id=1, source_target_pairs={{0,1},{1,0},{2,3},{3,2},{4,5},{5,4},{6,7},{7,6},{8,9},{9,8},{10,11... | collective-permute-start | bytes 1720328 | tf_op jit(solution)/shard_map/ppermute | solution.py:16
  78.3 30.6 %collective-permute-start.9 = (bf16[80,3584]{1,0:T(8,128)(2,1)S(1)}, bf16[80,3584]{1,0:T(8,128)(2,1)S(1)}, u32[]{:S(2)}, u32[]{:S(2)}) collective-permute-start(bf16[80,3584]{1,0:T(8,128)(2,1)S(1)} %collective-permute-done.8.refs_0_), channel_id=1, source_target_pairs={{0,1},{1,0},{2,3},{3,2},{4,5},{5,4},{6,7},{7,6},{8,9},{9,8},{10,11... | collective-permute-start | bytes 1720328 | tf_op jit(solution)/shard_map/ppermute | solution.py:16
  78.4 10.9 %collective-permute-start.27 = (bf16[80,3584]{1,0:T(8,128)(2,1)S(1)}, bf16[80,3584]{1,0:T(8,128)(2,1)S(1)}, u32[]{:S(2)}, u32[]{:S(2)}) collective-permute-start(bf16[80,3584]{1,0:T(8,128)(2,1)S(1)} %collective-permute-done.26.refs_2_), channel_id=1, source_target_pairs={{0,1},{1,0},{2,3},{3,2},{4,5},{5,4},{6,7},{7,6},{8,9},{9,8},{10,11... | collective-permute-start | bytes 1720328 | tf_op jit(solution)/shard_map/ppermute | solution.py:16
  88.6 10.6 %collective-permute-start.19 = (bf16[80,3584]{1,0:T(8,128)(2,1)S(1)}, bf16[80,3584]{1,0:T(8,128)(2,1)S(1)}, u32[]{:S(2)}, u32[]{:S(2)}) collective-permute-start(bf16[80,3584]{1,0:T(8,128)(2,1)S(1)} %collective-permute-done.18.refs_2_), channel_id=1, source_target_pairs={{0,1},{1,0},{2,3},{3,2},{4,5},{5,4},{6,7},{7,6},{8,9},{9,8},{10,11... | collective-permute-start | bytes 1720328 | tf_op jit(solution)/shard_map/ppermute | solution.py:16
  88.6 20.7 %collective-permute-start.11 = (bf16[80,3584]{1,0:T(8,128)(2,1)S(1)}, bf16[80,3584]{1,0:T(8,128)(2,1)S(1)}, u32[]{:S(2)}, u32[]{:S(2)}) collective-permute-start(bf16[80,3584]{1,0:T(8,128)(2,1)S(1)} %collective-permute-done.10.refs_2_), channel_id=1, source_target_pairs={{0,1},{1,0},{2,3},{3,2},{4,5},{5,4},{6,7},{7,6},{8,9},{9,8},{10,11... | collective-permute-start | bytes 1720328 | tf_op jit(solution)/shard_map/ppermute | solution.py:16
  89.3 29.5 %collective-permute-start.4 = (bf16[80,3584]{1,0:T(8,128)(2,1)S(1)}, bf16[80,3584]{1,0:T(8,128)(2,1)S(1)}, u32[]{:S(2)}, u32[]{:S(2)}) collective-permute-start(bf16[80,3584]{1,0:T(8,128)(2,1)S(1)} %get-tuple-element.27), channel_id=1, source_target_pairs={{0,1},{1,0},{2,3},{3,2},{4,5},{5,4},{6,7},{7,6},{8,9},{9,8},{10,11... | collective-permute-start | bytes 1720328 | tf_op jit(solution)/shard_map/ppermute | solution.py:16
  89.4 29.8 %collective-permute-start.6 = (bf16[80,3584]{1,0:T(8,128)(2,1)S(1)}, bf16[80,3584]{1,0:T(8,128)(2,1)S(1)}, u32[]{:S(2)}, u32[]{:S(2)}) collective-permute-start(bf16[80,3584]{1,0:T(8,128)(2,1)S(1)} %add_convert_fusion.10), channel_id=1, source_target_pairs={{0,2},{1,3},{2,0},{3,1},{4,6},{5,7},{6,4},{7,5},{8,10},{9,11},{10,... | collective-permute-start | bytes 1720328 | tf_op jit(solution)/shard_map/ppermute | solution.py:16
  99.3 20.3 %collective-permute-start.29 = (bf16[80,3584]{1,0:T(8,128)(2,1)S(1)}, bf16[80,3584]{1,0:T(8,128)(2,1)S(1)}, u32[]{:S(2)}, u32[]{:S(2)}) collective-permute-start(bf16[80,3584]{1,0:T(8,128)(2,1)S(1)} %get-tuple-element.44), channel_id=1, source_target_pairs={{0,1},{1,0},{2,3},{3,2},{4,5},{5,4},{6,7},{7,6},{8,9},{9,8},{10,11... | collective-permute-start | bytes 1720328 | tf_op jit(solution)/shard_map/ppermute | solution.py:16
  108.9 14.3 %collective-permute-start.28 = (bf16[80,3584]{1,0:T(8,128)(2,1)S(1)}, bf16[80,3584]{1,0:T(8,128)(2,1)S(1)}, u32[]{:S(2)}, u32[]{:S(2)}) collective-permute-start(bf16[80,3584]{1,0:T(8,128)(2,1)S(1)} %get-tuple-element.42), channel_id=1, source_target_pairs={{0,1},{1,0},{2,3},{3,2},{4,5},{5,4},{6,7},{7,6},{8,9},{9,8},{10,11... | collective-permute-start | bytes 1720328 | tf_op jit(solution)/shard_map/ppermute | solution.py:16
  109.3 10.8 %collective-permute-start.21 = (bf16[80,3584]{1,0:T(8,128)(2,1)S(1)}, bf16[80,3584]{1,0:T(8,128)(2,1)S(1)}, u32[]{:S(2)}, u32[]{:S(2)}) collective-permute-start(bf16[80,3584]{1,0:T(8,128)(2,1)S(1)} %get-tuple-element.39), channel_id=1, source_target_pairs={{0,1},{1,0},{2,3},{3,2},{4,5},{5,4},{6,7},{7,6},{8,9},{9,8},{10,11... | collective-permute-start | bytes 1720328 | tf_op jit(solution)/shard_map/ppermute | solution.py:16
  118.8 19.0 %collective-permute-start.20 = (bf16[80,3584]{1,0:T(8,128)(2,1)S(1)}, bf16[80,3584]{1,0:T(8,128)(2,1)S(1)}, u32[]{:S(2)}, u32[]{:S(2)}) collective-permute-start(bf16[80,3584]{1,0:T(8,128)(2,1)S(1)} %get-tuple-element.37), channel_id=1, source_target_pairs={{0,1},{1,0},{2,3},{3,2},{4,5},{5,4},{6,7},{7,6},{8,9},{9,8},{10,11... | collective-permute-start | bytes 1720328 | tf_op jit(solution)/shard_map/ppermute | solution.py:16
  119.2 2.6 %collective-permute-start.13 = (bf16[80,3584]{1,0:T(8,128)(2,1)S(1)}, bf16[80,3584]{1,0:T(8,128)(2,1)S(1)}, u32[]{:S(2)}, u32[]{:S(2)}) collective-permute-start(bf16[80,3584]{1,0:T(8,128)(2,1)S(1)} %get-tuple-element.34), channel_id=1, source_target_pairs={{0,1},{1,0},{2,3},{3,2},{4,5},{5,4},{6,7},{7,6},{8,9},{9,8},{10,11... | collective-permute-start | bytes 1720328 | tf_op jit(solution)/shard_map/ppermute | solution.py:16
  119.6 29.7 %collective-permute-start.12 = (bf16[80,3584]{1,0:T(8,128)(2,1)S(1)}, bf16[80,3584]{1,0:T(8,128)(2,1)S(1)}, u32[]{:S(2)}, u32[]{:S(2)}) collective-permute-start(bf16[80,3584]{1,0:T(8,128)(2,1)S(1)} %get-tuple-element.32), channel_id=1, source_target_pairs={{0,1},{1,0},{2,3},{3,2},{4,5},{5,4},{6,7},{7,6},{8,9},{9,8},{10,11... | collective-permute-start | bytes 1720328 | tf_op jit(solution)/shard_map/ppermute | solution.py:16
  120.1 15.9 %collective-permute-start.30 = (bf16[80,3584]{1,0:T(8,128)(2,1)S(1)}, bf16[80,3584]{1,0:T(8,128)(2,1)S(1)}, u32[]{:S(2)}, u32[]{:S(2)}) collective-permute-start(bf16[80,3584]{1,0:T(8,128)(2,1)S(1)} %add_convert_fusion.1), channel_id=1, source_target_pairs={{0,2},{1,3},{2,0},{3,1},{4,6},{5,7},{6,4},{7,5},{8,10},{9,11},{10,... | collective-permute-start | bytes 1720328 | tf_op jit(solution)/shard_map/ppermute | solution.py:16
  121.8 26.5 %collective-permute-start.22 = (bf16[80,3584]{1,0:T(8,128)(2,1)S(1)}, bf16[80,3584]{1,0:T(8,128)(2,1)S(1)}, u32[]{:S(2)}, u32[]{:S(2)}) collective-permute-start(bf16[80,3584]{1,0:T(8,128)(2,1)S(1)} %add_convert_fusion.4), channel_id=1, source_target_pairs={{0,2},{1,3},{2,0},{3,1},{4,6},{5,7},{6,4},{7,5},{8,10},{9,11},{10,... | collective-permute-start | bytes 1720328 | tf_op jit(solution)/shard_map/ppermute | solution.py:16
  123.3 36.6 %collective-permute-start.14 = (bf16[80,3584]{1,0:T(8,128)(2,1)S(1)}, bf16[80,3584]{1,0:T(8,128)(2,1)S(1)}, u32[]{:S(2)}, u32[]{:S(2)}) collective-permute-start(bf16[80,3584]{1,0:T(8,128)(2,1)S(1)} %add_convert_fusion.7), channel_id=1, source_target_pairs={{0,2},{1,3},{2,0},{3,1},{4,6},{5,7},{6,4},{7,5},{8,10},{9,11},{10,... | collective-permute-start | bytes 1720328 | tf_op jit(solution)/shard_map/ppermute | solution.py:16
  136.0 28.5 %collective-permute-start.7 = (bf16[80,3584]{1,0:T(8,128)(2,1)S(1)}, bf16[80,3584]{1,0:T(8,128)(2,1)S(1)}, u32[]{:S(2)}, u32[]{:S(2)}) collective-permute-start(bf16[80,3584]{1,0:T(8,128)(2,1)S(1)} %add_convert_fusion.9), channel_id=1, source_target_pairs={{0,16},{1,17},{2,18},{3,19},{4,20},{5,21},{6,22},{7,23},{8,24},{9,... | collective-permute-start | bytes 1720328 | tf_op jit(solution)/shard_map/ppermute | solution.py:26
  137.7 26.7 %collective-permute-start.31 = (bf16[80,3584]{1,0:T(8,128)(2,1)S(1)}, bf16[80,3584]{1,0:T(8,128)(2,1)S(1)}, u32[]{:S(2)}, u32[]{:S(2)}) collective-permute-start(bf16[80,3584]{1,0:T(8,128)(2,1)S(1)} %add_convert_fusion), channel_id=1, source_target_pairs={{0,28},{1,29},{2,30},{3,31},{4,24},{5,25},{6,26},{7,27},{8,20},{9,... | collective-permute-start | bytes 1720328 | tf_op jit(solution)/shard_map/ppermute | solution.py:26
  148.5 47.2 %collective-permute-start.23 = (bf16[80,3584]{1,0:T(8,128)(2,1)S(1)}, bf16[80,3584]{1,0:T(8,128)(2,1)S(1)}, u32[]{:S(2)}, u32[]{:S(2)}) collective-permute-start(bf16[80,3584]{1,0:T(8,128)(2,1)S(1)} %add_convert_fusion.3), channel_id=1, source_target_pairs={{0,24},{1,25},{2,26},{3,27},{4,28},{5,29},{6,30},{7,31},{8,16},{9,... | collective-permute-start | bytes 1720328 | tf_op jit(solution)/shard_map/ppermute | solution.py:26
  159.8 1.0 copy-start.11
  160.0 35.7 %collective-permute-start.15 = (bf16[80,3584]{1,0:T(8,128)(2,1)S(1)}, bf16[80,3584]{1,0:T(8,128)(2,1)S(1)}, u32[]{:S(2)}, u32[]{:S(2)}) collective-permute-start(bf16[80,3584]{1,0:T(8,128)(2,1)S(1)} %add_convert_fusion.6), channel_id=1, source_target_pairs={{0,20},{1,21},{2,22},{3,23},{4,16},{5,17},{6,18},{7,19},{8,28},{9,... | collective-permute-start | bytes 1720328 | tf_op jit(solution)/shard_map/ppermute | solution.py:26
  160.8 3.7 %collective-permute-start = (s32[2,128]{1,0:T(2,128)S(1)}, s32[2,128]{1,0:T(2,128)S(1)}, u32[]{:S(2)}, u32[]{:S(2)}) collective-permute-start(s32[2,128]{1,0:T(2,128)S(1)} %bitcast.41), channel_id=1, source_target_pairs={{0,16},{1,17},{2,18},{3,19},{4,20},{5,21},{6,22},{7,23},{8,24},{9,... | collective-permute-start | bytes 3080 | tf_op jit(solution)/shard_map/ppermute | solution.py:26

commit v2 on v1

v2 whole, which is shorter than its diff:
```python
import functools

import jax
import jax.numpy as jnp
from jax import lax
from jax.experimental import pallas as pl
from jax.experimental.pallas import tpu as pltpu
from jax.sharding import PartitionSpec as P

SPLIT = 4
MIB = 1 << 20


TIES = {
    ("plane", 3): [("plane", 2), ("pieces", 0)],
    ("chip", 2): [("pieces", 0)],
    ("chip", 1): [("pieces", 0)],
    ("chip", 3): [("pieces", 2)],
    ("pieces", 1): [("pieces", 2)],
}


def cut(experts, cap):
    return [(k, 0, cap) for k in range(experts)]


GIVEN = {
    "chip": ("plane",),
    "pieces": ("plane", "chip"),
    "chip_back": ("pieces",),
    "plane_back": ("pieces", "chip_back"),
}


def exchange(value, mask):
    count = lax.axis_size("ep")
    return lax.ppermute(value, "ep", [(i, i ^ mask) for i in range(count)])


def to_section_before(value, mask):
    sections, count = lax.axis_size("section"), lax.axis_size("ep")
    pairs = [
        (s * count + i, (s - 1) % sections * count + (i ^ mask))
        for s in range(sections)
        for i in range(count)
    ]
    return lax.ppermute(value, ("section", "ep"), pairs)


def column_tile(width):
    for parts in (4, 2):
        if width % (128 * parts) == 0:
            return width // parts
    return width


def fill_choices(own_ref, ids_ref, choice_ref, cap, experts):
    top, tokens = ids_ref.shape
    expert = lax.broadcasted_iota(jnp.int32, (experts, tokens), 0) ^ own_ref[0]
    named = ids_ref[0:1, :] == expert
    for k in range(1, top):
        named = named | (ids_ref[k : k + 1, :] == expert)
    member = jnp.where(named, 1.0, 0.0)
    earlier = lax.broadcasted_iota(jnp.int32, (tokens, tokens), 0) < lax.broadcasted_iota(
        jnp.int32, (tokens, tokens), 1
    )
    slots = jnp.dot(
        member.astype(jnp.bfloat16),
        jnp.where(earlier, 1.0, 0.0).astype(jnp.bfloat16),
        preferred_element_type=jnp.float32,
    )
    slots = jnp.where(named, slots, -1.0)
    place = lax.broadcasted_iota(jnp.int32, (cap, tokens), 0).astype(jnp.float32)
    for k in range(experts):
        choice_ref[k * cap : (k + 1) * cap, :] = jnp.where(
            place == slots[k : k + 1, :], 1.0, 0.0
        ).astype(choice_ref.dtype)


def dispatch_kernel(cap, experts, units, own_ref, ids_ref, gates_ref, rows_ref, *refs):
    outs, (choice_ref, weight_ref) = refs[: len(units)], refs[len(units) :]

    @pl.when(pl.program_id(0) == 0)
    def _():
        fill_choices(own_ref, ids_ref, choice_ref, cap, experts)
        top, tokens = ids_ref.shape
        for k in range(experts):
            expert = own_ref[0] ^ k
            gate = jnp.zeros((1, tokens), jnp.float32)
            for j in range(top):
                gate = jnp.where(ids_ref[j : j + 1, :] == expert, gates_ref[j : j + 1, :], gate)
            chosen = choice_ref[k * cap : (k + 1) * cap, :].astype(jnp.float32)
            weight_ref[k * cap : (k + 1) * cap, :] = jnp.sum(chosen * gate, axis=1, keepdims=True)

    picked = jnp.dot(choice_ref[...], rows_ref[...], preferred_element_type=jnp.float32)
    payload = (picked * weight_ref[...]).astype(jnp.bfloat16)
    for out_ref, (k, first, count) in zip(outs, units):
        out_ref[...] = payload[k * cap + first : k * cap + first + count, :]


def dispatch(own, ids, gates, rows, cap, experts, units):
    tokens, width = rows.shape
    tile = column_tile(width)
    whole = pl.BlockSpec(ids.shape, lambda i, own: (0, 0))
    return pl.pallas_call(
        functools.partial(dispatch_kernel, cap, experts, units),
        grid_spec=pltpu.PrefetchScalarGridSpec(
            num_scalar_prefetch=1,
            grid=(width // tile,),
            in_specs=[whole, whole, pl.BlockSpec((tokens, tile), lambda i, own: (0, i))],
            out_specs=[pl.BlockSpec((count, tile), lambda i, own: (0, i)) for _, _, count in units],
            scratch_shapes=[
                pltpu.VMEM((experts * cap, tokens), jnp.bfloat16),
                pltpu.VMEM((experts * cap, 1), jnp.float32),
            ],
        ),
        out_shape=[jax.ShapeDtypeStruct((count, width), jnp.bfloat16) for _, _, count in units],
        compiler_params=pltpu.CompilerParams(vmem_limit_bytes=16 * MIB),
        cost_estimate=pl.CostEstimate(
            flops=1000, bytes_accessed=1000, transcendentals=0
        ),
        name="dispatch",
    )(own, ids, gates, rows)


def combine_kernel(cap, experts, units, own_ref, ids_ref, *refs):
    rows, out_ref, choice_ref = refs[: len(units)], refs[-2], refs[-1]

    @pl.when(pl.program_id(0) == 0)
    def _():
        fill_choices(own_ref, ids_ref, choice_ref, cap, experts)

    total = None
    for rows_ref, (k, first, count) in zip(rows, units):
        part = lax.dot_general(
            choice_ref[k * cap + first : k * cap + first + count, :],
            rows_ref[...],
            (((0,), (0,)), ((), ())),
            preferred_element_type=jnp.float32,
        )
        total = part if total is None else total + part
    out_ref[...] = total.astype(jnp.bfloat16)


def combine(own, ids, returned, cap, experts, units):
    width, tokens = returned[0].shape[1], ids.shape[1]
    tile = column_tile(width)
    return pl.pallas_call(
        functools.partial(combine_kernel, cap, experts, units),
        grid_spec=pltpu.PrefetchScalarGridSpec(
            num_scalar_prefetch=1,
            grid=(width // tile,),
            in_specs=[pl.BlockSpec(ids.shape, lambda i, own: (0, 0))]
            + [pl.BlockSpec((count, tile), lambda i, own: (0, i)) for _, _, count in units],
            out_specs=pl.BlockSpec((tokens, tile), lambda i, own: (0, i)),
            scratch_shapes=[pltpu.VMEM((experts * cap, tokens), jnp.bfloat16)],
        ),
        out_shape=jax.ShapeDtypeStruct((tokens, width), jnp.bfloat16),
        compiler_params=pltpu.CompilerParams(vmem_limit_bytes=16 * MIB),
        cost_estimate=pl.CostEstimate(
            flops=1000, bytes_accessed=1000, transcendentals=0
        ),
        name="combine",
    )(own, ids, *returned)


def pieces_kernel(parts, first, source_ref, *refs):
    blocks, saved, weights, outs = refs[:2], refs[2:6], refs[6:12], refs[12:14]
    here, sem = refs[14:]
    count, width = blocks[0].shape
    tile = width // parts
    copies = []
    for n, ref in enumerate(saved):
        for j in range(2):
            copies.append(
                pltpu.make_async_copy(
                    ref.at[source_ref[n // 2, j], pl.ds(first, count)],
                    here.at[n, pl.ds(j * count, count)],
                    sem.at[n, j],
                )
            )
    for copy in copies:
        copy.start()
    across = (((1,), (1,)), ((), ()))
    rows = jnp.concatenate([block[...] for block in blocks], axis=0)
    totals = [
        lax.dot_general(rows, weights[3 * n + 2][...], across, preferred_element_type=jnp.float32)
        for n in range(2)
    ]
    for copy in copies:
        copy.wait()
    grads = []
    for n in range(2):
        g = here[2 * n].astype(jnp.float32)
        u = here[2 * n + 1].astype(jnp.float32)
        s = jax.nn.sigmoid(g)
        grads.append((totals[n] * u * s * (1.0 + g * (1.0 - s))).astype(jnp.bfloat16))
        grads.append((totals[n] * g * s).astype(jnp.bfloat16))
    for i in range(parts):
        at = pl.ds(i * tile, tile)
        part = None
        for grad, weight in zip(grads, (weights[0], weights[1], weights[3], weights[4])):
            term = lax.dot_general(grad, weight[at, :], across, preferred_element_type=jnp.float32)
            part = term if part is None else part + term
        part = part.astype(jnp.bfloat16)
        for j in range(2):
            outs[j][:, at] = part[j * count : (j + 1) * count, :]


def pieces(first, source, blocks, saved, weights):
    count, width = blocks[0].shape
    hidden = weights[2].shape[0]
    parts = width // 512 if width % 512 == 0 else 1
    anywhere = pl.BlockSpec(memory_space=pl.ANY)
    near = pl.BlockSpec(memory_space=pltpu.VMEM)
    return pl.pallas_call(
        functools.partial(pieces_kernel, parts, first),
        in_specs=[pl.BlockSpec(memory_space=pltpu.SMEM)] + [near] * 2 + [anywhere] * 4 + [near] * 6,
        out_specs=[near] * 2,
        out_shape=[jax.ShapeDtypeStruct((count, width), jnp.bfloat16)] * 2,
        scratch_shapes=[
            pltpu.VMEM((4, 2 * count, hidden), jnp.bfloat16),
            pltpu.SemaphoreType.DMA((4, 2)),
        ],
        compiler_params=pltpu.CompilerParams(vmem_limit_bytes=20 * MIB),
        cost_estimate=pl.CostEstimate(flops=1000, bytes_accessed=1000, transcendentals=0),
        name="pieces",
    )(source, *blocks, *saved, *weights)


def after(value, *others):
    if isinstance(value, (list, tuple)):
        return list(lax.optimization_barrier((tuple(value), *others))[0])
    return lax.optimization_barrier((value, *others))[0]


def first_of(value):
    return value[0] if isinstance(value, (list, tuple)) else value


def added(a, b):
    return (a.astype(jnp.float32) + b.astype(jnp.float32)).astype(jnp.bfloat16)


def local(grad_output, route_ids, route_gates, gate_pre, up_pre, w_gate, w_up, w_down):
    experts = lax.axis_size("ep") // SPLIT
    me = lax.axis_index("ep")
    own, seat = me // SPLIT, me % SPLIT
    cap = gate_pre.shape[3]
    gate_saved, up_saved = gate_pre[0, 0], up_pre[0, 0]
    spare = -cap % 16
    if spare:
        gate_saved = jnp.pad(gate_saved, ((0, 0), (0, spare), (0, 0)))
        up_saved = jnp.pad(up_saved, ((0, 0), (0, spare), (0, 0)))
        cap += spare
    ids = route_ids[0].T
    own = own.astype(jnp.int32).reshape(1)
    units = cut(experts, cap)
    outgoing = dispatch(own, ids, route_gates[0].T, grad_output[0], cap, experts, units)
    weights = [w_gate[0, 0], w_up[0, 0], w_down[0, 0]]
    weights = weights + [exchange(w, 1) for w in weights]
    values = {}

    def step(kind, i):
        if (kind, i) not in values:
            k, first, _ = units[i]
            given = [step(name, i) for name in GIVEN[kind]] if kind != "plane" else [outgoing[i]]
            ties = [first_of(step(*t)) for t in TIES.get((kind, i), ()) if t[1] < len(units)]
            if ties:
                given[0] = after(given[0], *ties)
            if (kind, i) == ("pieces", 0):
                given[0] = after(given[0], ids_after)
            with jax.named_scope(f"{kind}_{i}"):
                values[kind, i] = work(kind, k, first, given)
        return values[kind, i]

    def work(kind, k, first, given):
        if kind == "plane":
            return exchange(given[0], k * SPLIT) if k else given[0]
        if kind == "chip":
            return exchange(given[0], 2)
        if kind == "pieces":
            source = ((own ^ k) * SPLIT + (seat ^ jnp.array([0, 2], jnp.int32))).astype(jnp.int32)
            return pieces(first, jnp.stack([source, source // 2]), given, saved, weights)
        if kind == "chip_back":
            return exchange(given[0][1], 2)
        return to_section_before(added(given[0][0], given[1]), k * SPLIT)

    with jax.named_scope("ids"):
        ids_after = to_section_before(after(ids, outgoing[0]), 0)
    other_core = [
        lax.dynamic_index_in_dim(
            v.reshape(experts * SPLIT // 2, 2, *v.shape[1:]), 1 - seat % 2, 1, keepdims=False
        )
        for v in (after(gate_saved, outgoing[0]), after(up_saved, outgoing[0]))
    ]
    saved = [gate_saved, up_saved] + [exchange(v, 1) for v in other_core]
    returned = [step("plane_back", i) for i in range(len(units))]
    return combine(own, ids_after, returned, cap, experts, units)[None]


def solution(mesh):
    placed = (
        P("section", "ep", None),
        P("section", "ep", None),
        P("section", "ep", None),
        P("section", "ep", None, None, None),
        P("section", "ep", None, None, None),
        P("section", "ep", None, None),
        P("section", "ep", None, None),
        P("section", "ep", None, None),
    )
    return jax.shard_map(
        local, mesh=mesh, in_specs=placed, out_specs=P("section", "ep", None), check_vma=False
    )
```

time: 199 us -> 163 us (0.82)
  the two profiles are of different devices: /device:TPU:0 before, /device:TPU:16 now
where the time goes in v2:
time: 163 us
  waiting for transfers between devices  94 us (58%)
  Pallas kernels  32.9 us (20%)
  starting transfers between devices  23.6 us (14%)
  local copies, waits for them, and re-layouts  11.3 us (7%)
    ppermute x16, waiting for transfers between devices, exchange(): return lax.ppermute(value, 'ep', [(i, i ^ mask) for i in range(count)])  66 us
    pallas_call x4, Pallas kernels, pieces(): pl.pallas_call(functools.partial(pieces_kernel, parts, first), in_specs=[...  28.1 us
    ppermute x5, waiting for transfers between devices, to_section_before(): return lax.ppermute(value, ('section', 'ep'), pairs)  28 us
    ppermute x16, starting transfers between devices, exchange(): return lax.ppermute(value, 'ep', [(i, i ^ mask) for i in range(count)])  14.9 us
    unnamed x26, local copies, waits for them, and re-layouts  9.34 us
    ppermute x5, starting transfers between devices, to_section_before(): return lax.ppermute(value, ('section', 'ep'), pairs)  8.69 us
  transfers between devices with their start and end apart: 21, of which 13 were waited for; matrix products, arithmetic and copies ran while one was open for 2% of the time, Pallas kernels for 18%

profile of v2, /device:TPU:16, one launch (start us, length us, event | category | flops | bytes accessed | tf_op | source)
XLA Modules:
  0.0 162.7 jit_solution(31646881330692981)
XLA Ops:
  0.0 0.0 collective-permute-start.4
  0.0 0.5 collective-permute-start.5
  0.5 0.1 collective-permute-start.6
  0.6 1.2 copy-done.7
  1.8 0.7 copy-done.8
  2.4 0.7 copy-done.9
  3.1 1.8 %dispatch.1 = (bf16[80,3584]{1,0:T(8,128)(2,1)S(1)}, bf16[80,3584]{1,0:T(8,128)(2,1)S(1)}, bf16[80,3584]{1,0:T(8,128)(2,1)S(1)}, bf16[80,3584]{1,0:T(8,128)(2,1)S(1)}) custom-call(s32[1]{0:T(128)} %bitcast.own_ref, s32[2,128]{1,0:T(2,128)S(1)} %bitcast.71, f32[2,128]{1,0:T(2,128)S(1)} %bitcast.70, bf16[128,3584]{1,0:T(8,128)(2,1)S(1)} %bitcast.69), custom_call_target="tpu_custom_call" | custom-call | flops 1000 | bytes 1000 | tf_op jit(solution)/shard_map/dispatch/pallas_call | solution.py:105
  4.9 0.0 copy-start.11
  4.9 0.8 copy-done.11
  5.7 0.8 copy-done.12
  6.6 1.0 dynamic-slice_bitcast_fusion
  7.6 0.5 collective-permute-start.3
  8.1 1.5 collective-permute-start
  9.6 2.0 %collective-permute-done.ids_ref = s32[2,128]{1,0:T(2,128)S(1)} collective-permute-done((s32[2,128]{1,0:T(2,128)S(1)}, s32[2,128]{1,0:T(2,128)S(1)}, u32[]{:S(2)}, u32[]{:S(2)}) %collective-permute-start) | collective-permute-done | bytes 1056 | tf_op jit(solution)/shard_map/ids/ppermute | solution.py:47
  11.6 1.5 collective-permute-start.1
  13.1 1.0 dynamic-slice_bitcast_fusion.1
  14.1 0.0 collective-permute-done.3.refs_5_
  14.1 0.1 collective-permute-start.2
  14.2 1.6 collective-permute-done.2.refs_4_
  15.8 0.3 collective-permute-start.10
  16.2 9.3 %collective-permute-done.1.refs_1_ = bf16[80,3584]{1,0:T(8,128)(2,1)S(1)} collective-permute-done((bf16[80,3584]{1,0:T(8,128)(2,1)S(1)}, bf16[80,3584]{1,0:T(8,128)(2,1)S(1)}, u32[]{:S(2)}, u32[]{:S(2)}) %collective-permute-start.1) | collective-permute-done | bytes 573472 | tf_op jit(solution)/shard_map/chip_0/ppermute | solution.py:37
  25.5 1.6 collective-permute-start.9
  27.1 0.0 collective-permute-done.4.refs_9_
  27.1 0.0 collective-permute-done.6.refs_11_
  27.1 0.0 copy-start.1
  27.1 1.5 copy-done.1
  28.6 1.5 copy-done.2
  30.1 1.1 copy-done.3
  31.2 1.1 copy-done.5
  32.3 7.1 %pieces.4 = (bf16[80,3584]{1,0:T(8,128)(2,1)S(1)}, bf16[80,3584]{1,0:T(8,128)(2,1)S(1)}) custom-call(s32[2,2]{1,0:T(2,128)S(1)} %pad_add_fusion.source_ref, bf16[80,3584]{1,0:T(8,128)(2,1)S(1)} %get-tuple-element.28.refs_0_, bf16[80,3584]{1,0:T(8,128)(2,1)S(1)} %collective-permute-done.1.refs_1_, bf16[16,80,256]{2,1,0:T(8,128)(2,1)S(1)} %bitcast.60, ...), custom_call_target="tpu_custom_call" | custom-call | flops 1000 | bytes 1000 | tf_op jit(solution)/shard_map/pieces_0/pieces/pallas_call | solution.py:216
  39.4 2.0 %collective-permute-done.10.refs_0_ = bf16[80,3584]{1,0:T(8,128)(2,1)S(1)} collective-permute-done((bf16[80,3584]{1,0:T(8,128)(2,1)}, bf16[80,3584]{1,0:T(8,128)(2,1)S(1)}, u32[]{:S(2)}, u32[]{:S(2)}) %collective-permute-start.10) | collective-permute-done | bytes 573472 | tf_op jit(solution)/shard_map/plane_2/ppermute | solution.py:37
  41.4 2.6 %collective-permute-start.17 = (bf16[80,3584]{1,0:T(8,128)(2,1)S(1)}, bf16[80,3584]{1,0:T(8,128)(2,1)S(1)}, u32[]{:S(2)}, u32[]{:S(2)}) collective-permute-start(bf16[80,3584]{1,0:T(8,128)(2,1)S(1)} %get-tuple-element.43), channel_id=1, source_target_pairs={{0,12},{1,13},{2,14},{3,15},{4,8},{5,9},{6,10},{7,11},{8,4},{9,5},... | collective-permute-start | bytes 1720328 | tf_op jit(solution)/shard_map/plane_3/ppermute | solution.py:37
  44.0 0.5 collective-permute-start.11
  44.5 17.8 %collective-permute-done.9.refs_0_ = bf16[80,3584]{1,0:T(8,128)(2,1)S(1)} collective-permute-done((bf16[80,3584]{1,0:T(8,128)(2,1)}, bf16[80,3584]{1,0:T(8,128)(2,1)S(1)}, u32[]{:S(2)}, u32[]{:S(2)}) %collective-permute-start.9) | collective-permute-done | bytes 573472 | tf_op jit(solution)/shard_map/plane_1/ppermute | solution.py:37
  62.3 1.5 collective-permute-start.12
  63.7 0.5 collective-permute-start.7
  64.4 0.0 collective-permute-done.11.refs_1_
  64.4 7.0 %pieces.5 = (bf16[80,3584]{1,0:T(8,128)(2,1)S(1)}, bf16[80,3584]{1,0:T(8,128)(2,1)S(1)}) custom-call(s32[2,2]{1,0:T(2,128)S(1)} %pad_add_fusion.2.source_ref, bf16[80,3584]{1,0:T(8,128)(2,1)S(1)} %collective-permute-done.10.refs_0_, bf16[80,3584]{1,0:T(8,128)(2,1)S(1)} %collective-permute-done.11.refs_1_, bf16[16,80,256]{2,1,0:T(8,128)(2,1)S(1)} %bitcast.61, ...), custom_call_target="tpu_custom_call" | custom-call | flops 1000 | bytes 1000 | tf_op jit(solution)/shard_map/pieces_2/pieces/pallas_call | solution.py:216
  71.4 0.0 collective-permute-done.17.refs_0_
  71.4 1.6 collective-permute-start.18
  73.0 0.5 collective-permute-start.15
  73.5 4.6 %collective-permute-done.12.refs_1_ = bf16[80,3584]{1,0:T(8,128)(2,1)S(1)} collective-permute-done((bf16[80,3584]{1,0:T(8,128)(2,1)S(1)}, bf16[80,3584]{1,0:T(8,128)(2,1)S(1)}, u32[]{:S(2)}, u32[]{:S(2)}) %collective-permute-start.12) | collective-permute-done | bytes 573472 | tf_op jit(solution)/shard_map/chip_1/ppermute | solution.py:37
  78.2 7.0 %pieces.6 = (bf16[80,3584]{1,0:T(8,128)(2,1)S(1)}, bf16[80,3584]{1,0:T(8,128)(2,1)S(1)}) custom-call(s32[2,2]{1,0:T(2,128)S(1)} %pad_add_fusion.1.source_ref, bf16[80,3584]{1,0:T(8,128)(2,1)S(1)} %collective-permute-done.9.refs_0_, bf16[80,3584]{1,0:T(8,128)(2,1)S(1)} %collective-permute-done.12.refs_1_, bf16[16,80,256]{2,1,0:T(8,128)(2,1)S(1)} %bitcast.62, ...), custom_call_target="tpu_custom_call" | custom-call | flops 1000 | bytes 1000 | tf_op jit(solution)/shard_map/pieces_1/pieces/pallas_call | solution.py:216
  85.2 1.6 collective-permute-start.13
  86.7 3.7 %collective-permute-done.7 = bf16[80,3584]{1,0:T(8,128)(2,1)S(1)} collective-permute-done((bf16[80,3584]{1,0:T(8,128)(2,1)S(1)}, bf16[80,3584]{1,0:T(8,128)(2,1)S(1)}, u32[]{:S(2)}, u32[]{:S(2)}) %collective-permute-start.7) | collective-permute-done | bytes 573472 | tf_op jit(solution)/shard_map/chip_back_0/ppermute | solution.py:37
  90.5 0.1 add_convert_fusion.3
  90.6 1.6 collective-permute-start.8
  92.2 10.6 %collective-permute-done.18.refs_1_ = bf16[80,3584]{1,0:T(8,128)(2,1)S(1)} collective-permute-done((bf16[80,3584]{1,0:T(8,128)(2,1)S(1)}, bf16[80,3584]{1,0:T(8,128)(2,1)S(1)}, u32[]{:S(2)}, u32[]{:S(2)}) %collective-permute-start.18) | collective-permute-done | bytes 573472 | tf_op jit(solution)/shard_map/chip_3/ppermute | solution.py:37
  102.7 7.0 %pieces.7 = (bf16[80,3584]{1,0:T(8,128)(2,1)S(1)}, bf16[80,3584]{1,0:T(8,128)(2,1)S(1)}) custom-call(s32[2,2]{1,0:T(2,128)S(1)} %pad_add_fusion.3.source_ref, bf16[80,3584]{1,0:T(8,128)(2,1)S(1)} %collective-permute-done.17.refs_0_, bf16[80,3584]{1,0:T(8,128)(2,1)S(1)} %collective-permute-done.18.refs_1_, bf16[16,80,256]{2,1,0:T(8,128)(2,1)S(1)} %bitcast.63, ...), custom_call_target="tpu_custom_call" | custom-call | flops 1000 | bytes 1000 | tf_op jit(solution)/shard_map/pieces_3/pieces/pallas_call | solution.py:216
  109.8 1.6 collective-permute-start.19
  111.3 3.7 %collective-permute-done.15 = bf16[80,3584]{1,0:T(8,128)(2,1)S(1)} collective-permute-done((bf16[80,3584]{1,0:T(8,128)(2,1)S(1)}, bf16[80,3584]{1,0:T(8,128)(2,1)S(1)}, u32[]{:S(2)}, u32[]{:S(2)}) %collective-permute-start.15) | collective-permute-done | bytes 573472 | tf_op jit(solution)/shard_map/chip_back_2/ppermute | solution.py:37
  115.0 0.1 add_convert_fusion.1
  115.2 1.1 collective-permute-start.16
  116.3 9.9 %collective-permute-done.13 = bf16[80,3584]{1,0:T(8,128)(2,1)S(1)} collective-permute-done((bf16[80,3584]{1,0:T(8,128)(2,1)S(1)}, bf16[80,3584]{1,0:T(8,128)(2,1)S(1)}, u32[]{:S(2)}, u32[]{:S(2)}) %collective-permute-start.13) | collective-permute-done | bytes 573472 | tf_op jit(solution)/shard_map/chip_back_1/ppermute | solution.py:37
  126.2 0.1 add_convert_fusion.2
  126.3 3.1 %collective-permute-start.14 = (bf16[80,3584]{1,0:T(8,128)(2,1)S(1)}, bf16[80,3584]{1,0:T(8,128)(2,1)S(1)}, u32[]{:S(2)}, u32[]{:S(2)}) collective-permute-start(bf16[80,3584]{1,0:T(8,128)(2,1)S(1)} %add_convert_fusion.2), channel_id=1, source_target_pairs={{0,20},{1,21},{2,22},{3,23},{4,16},{5,17},{6,18},{7,19},{8,28},{9,... | collective-permute-start | bytes 1720328 | tf_op jit(solution)/shard_map/plane_back_1/ppermute | solution.py:47
  129.4 2.9 %collective-permute-done.19 = bf16[80,3584]{1,0:T(8,128)(2,1)S(1)} collective-permute-done((bf16[80,3584]{1,0:T(8,128)(2,1)S(1)}, bf16[80,3584]{1,0:T(8,128)(2,1)S(1)}, u32[]{:S(2)}, u32[]{:S(2)}) %collective-permute-start.19) | collective-permute-done | bytes 573472 | tf_op jit(solution)/shard_map/chip_back_3/ppermute | solution.py:37
  132.3 0.1 add_convert_fusion
  132.5 1.3 collective-permute-start.20
  133.8 0.0 collective-permute-done.8.refs_0_
  133.8 0.0 collective-permute-done.16.refs_2_
  133.8 8.6 %collective-permute-done.14.refs_1_ = bf16[80,3584]{1,0:T(8,128)(2,1)S(1)} collective-permute-done((bf16[80,3584]{1,0:T(8,128)(2,1)S(1)}, bf16[80,3584]{1,0:T(8,128)(2,1)S(1)}, u32[]{:S(2)}, u32[]{:S(2)}) %collective-permute-start.14) | collective-permute-done | bytes 573472 | tf_op jit(solution)/shard_map/plane_back_1/ppermute | solution.py:47
  142.4 17.3 %collective-permute-done.20.refs_3_ = bf16[80,3584]{1,0:T(8,128)(2,1)S(1)} collective-permute-done((bf16[80,3584]{1,0:T(8,128)(2,1)S(1)}, bf16[80,3584]{1,0:T(8,128)(2,1)S(1)}, u32[]{:S(2)}, u32[]{:S(2)}) %collective-permute-start.20) | collective-permute-done | bytes 573472 | tf_op jit(solution)/shard_map/plane_back_3/ppermute | solution.py:47
  159.7 3.0 %combine.1 = bf16[128,3584]{1,0:T(8,128)(2,1)} custom-call(s32[1]{0:T(128)} %bitcast.own_ref, s32[2,128]{1,0:T(2,128)S(1)} %collective-permute-done.ids_ref, bf16[80,3584]{1,0:T(8,128)(2,1)S(1)} %collective-permute-done.8.refs_0_, bf16[80,3584]{1,0:T(8,128)(2,1)S(1)} %collective-permute-done.14.refs_1_, ...), custom_call_target="tpu_custom_call" | custom-call | flops 1000 | bytes 1000 | tf_op jit(solution)/shard_map/combine/pallas_call | solution.py:148
  (24 shorter events, 0.1 us)
Async XLA Ops:
  0.0 8.1 %copy-start.10 = (s32[1,128,2]{1,2,0:T(2,128)S(1)}, s32[1,128,2]{1,2,0:T(2,128)}, u32[]{:S(2)}) copy-start(s32[1,128,2]{1,2,0:T(2,128)} %param.13) | copy-start | bytes 3076
  0.0 27.1 %collective-permute-start.4 = (bf16[3584,256]{1,0:T(8,128)(2,1)}, bf16[3584,256]{1,0:T(8,128)(2,1)}, u32[]{:S(2)}, u32[]{:S(2)}) collective-permute-start(bf16[3584,256]{1,0:T(8,128)(2,1)} %bitcast.44), channel_id=1, source_target_pairs={{0,1},{1,0},{2,3},{3,2},{4,5},{5,4},{6,7},{7,6},{8,9},{9,8},{10,11... | collective-permute-start | bytes 5505032 | tf_op jit(solution)/shard_map/ppermute | solution.py:37
  0.0 27.1 %collective-permute-start.5 = (bf16[3584,256]{1,0:T(8,128)(2,1)}, bf16[3584,256]{1,0:T(8,128)(2,1)}, u32[]{:S(2)}, u32[]{:S(2)}) collective-permute-start(bf16[3584,256]{1,0:T(8,128)(2,1)} %bitcast.49), channel_id=1, source_target_pairs={{0,1},{1,0},{2,3},{3,2},{4,5},{5,4},{6,7},{7,6},{8,9},{9,8},{10,11... | collective-permute-start | bytes 5505032 | tf_op jit(solution)/shard_map/ppermute | solution.py:37
  0.5 26.6 %collective-permute-start.6 = (bf16[256,3584]{1,0:T(8,128)(2,1)}, bf16[256,3584]{1,0:T(8,128)(2,1)}, u32[]{:S(2)}, u32[]{:S(2)}) collective-permute-start(bf16[256,3584]{1,0:T(8,128)(2,1)} %bitcast.54), channel_id=1, source_target_pairs={{0,1},{1,0},{2,3},{3,2},{4,5},{5,4},{6,7},{7,6},{8,9},{9,8},{10,11... | collective-permute-start | bytes 5505032 | tf_op jit(solution)/shard_map/ppermute | solution.py:37
  0.6 1.2 copy-start.7
  1.8 0.7 copy-start.8
  2.4 0.7 copy-start.9
  3.1 24.0 %copy-start = (bf16[1,1,3584,256]{3,2,1,0:T(8,128)(2,1)S(1)}, bf16[1,1,3584,256]{3,2,1,0:T(8,128)(2,1)}, u32[]{:S(2)}) copy-start(bf16[1,1,3584,256]{3,2,1,0:T(8,128)(2,1)} %param.17) | copy-start | bytes 5505028
  4.9 0.8 copy-start.11
  5.7 0.8 copy-start.12
  7.6 6.6 %collective-permute-start.3 = (bf16[8,80,256]{2,1,0:T(8,128)(2,1)S(1)}, bf16[8,80,256]{2,1,0:T(8,128)(2,1)S(1)}, u32[]{:S(2)}, u32[]{:S(2)}) collective-permute-start(bf16[8,80,256]{2,1,0:T(8,128)(2,1)S(1)} %dynamic-slice_bitcast_fusion), channel_id=1, source_target_pairs={{0,1},{1,0},{2,3},{3,2},{4,5},{5,4},{6,7},{7,6},{8,9},{9,8},{10,11... | collective-permute-start | bytes 983048 | tf_op jit(solution)/shard_map/ppermute | solution.py:37
  8.1 3.6 %collective-permute-start = (s32[2,128]{1,0:T(2,128)S(1)}, s32[2,128]{1,0:T(2,128)S(1)}, u32[]{:S(2)}, u32[]{:S(2)}) collective-permute-start(s32[2,128]{1,0:T(2,128)S(1)} %bitcast.72), channel_id=1, source_target_pairs={{0,16},{1,17},{2,18},{3,19},{4,20},{5,21},{6,22},{7,23},{8,24},{9,... | collective-permute-start | bytes 3080 | tf_op jit(solution)/shard_map/ids/ppermute | solution.py:47
  11.6 13.8 %collective-permute-start.1 = (bf16[80,3584]{1,0:T(8,128)(2,1)S(1)}, bf16[80,3584]{1,0:T(8,128)(2,1)S(1)}, u32[]{:S(2)}, u32[]{:S(2)}) collective-permute-start(bf16[80,3584]{1,0:T(8,128)(2,1)S(1)} %get-tuple-element.28.refs_0_), channel_id=1, source_target_pairs={{0,2},{1,3},{2,0},{3,1},{4,6},{5,7},{6,4},{7,5},{8,10},{9,11},{10,... | collective-permute-start | bytes 1720328 | tf_op jit(solution)/shard_map/chip_0/ppermute | solution.py:37
  14.1 1.7 %collective-permute-start.2 = (bf16[8,80,256]{2,1,0:T(8,128)(2,1)S(1)}, bf16[8,80,256]{2,1,0:T(8,128)(2,1)S(1)}, u32[]{:S(2)}, u32[]{:S(2)}) collective-permute-start(bf16[8,80,256]{2,1,0:T(8,128)(2,1)S(1)} %dynamic-slice_bitcast_fusion.1), channel_id=1, source_target_pairs={{0,1},{1,0},{2,3},{3,2},{4,5},{5,4},{6,7},{7,6},{8,9},{9,8},{10,11... | collective-permute-start | bytes 983048 | tf_op jit(solution)/shard_map/ppermute | solution.py:37
  15.8 25.5 %collective-permute-start.10 = (bf16[80,3584]{1,0:T(8,128)(2,1)}, bf16[80,3584]{1,0:T(8,128)(2,1)S(1)}, u32[]{:S(2)}, u32[]{:S(2)}) collective-permute-start(bf16[80,3584]{1,0:T(8,128)(2,1)} %copy-done.12), channel_id=1, source_target_pairs={{0,8},{1,9},{2,10},{3,11},{4,12},{5,13},{6,14},{7,15},{8,0},{9,1},... | collective-permute-start | bytes 1720328 | tf_op jit(solution)/shard_map/plane_2/ppermute | solution.py:37
  25.5 36.8 %collective-permute-start.9 = (bf16[80,3584]{1,0:T(8,128)(2,1)}, bf16[80,3584]{1,0:T(8,128)(2,1)S(1)}, u32[]{:S(2)}, u32[]{:S(2)}) collective-permute-start(bf16[80,3584]{1,0:T(8,128)(2,1)} %copy-done.11), channel_id=1, source_target_pairs={{0,4},{1,5},{2,6},{3,7},{4,0},{5,1},{6,2},{7,3},{8,12},{9,13},{10,... | collective-permute-start | bytes 1720328 | tf_op jit(solution)/shard_map/plane_1/ppermute | solution.py:37
  27.1 1.5 copy-start.1
  28.6 1.5 copy-start.2
  30.1 1.1 copy-start.3
  31.2 1.1 copy-start.5
  32.3 32.1 %copy-start.4 = (bf16[1,1,16,80,256]{4,3,2,1,0:T(8,128)(2,1)S(1)}, bf16[1,1,16,80,256]{4,3,2,1,0:T(8,128)(2,1)}, u32[]{:S(2)}) copy-start(bf16[1,1,16,80,256]{4,3,2,1,0:T(8,128)(2,1)} %param.15) | copy-start | bytes 1966084
  32.3 32.1 %copy-start.6 = (bf16[1,1,16,80,256]{4,3,2,1,0:T(8,128)(2,1)S(1)}, bf16[1,1,16,80,256]{4,3,2,1,0:T(8,128)(2,1)}, u32[]{:S(2)}) copy-start(bf16[1,1,16,80,256]{4,3,2,1,0:T(8,128)(2,1)} %param.16) | copy-start | bytes 1966084
  41.4 30.1 %collective-permute-start.17 = (bf16[80,3584]{1,0:T(8,128)(2,1)S(1)}, bf16[80,3584]{1,0:T(8,128)(2,1)S(1)}, u32[]{:S(2)}, u32[]{:S(2)}) collective-permute-start(bf16[80,3584]{1,0:T(8,128)(2,1)S(1)} %get-tuple-element.43), channel_id=1, source_target_pairs={{0,12},{1,13},{2,14},{3,15},{4,8},{5,9},{6,10},{7,11},{8,4},{9,5},... | collective-permute-start | bytes 1720328 | tf_op jit(solution)/shard_map/plane_3/ppermute | solution.py:37
  44.0 20.4 %collective-permute-start.11 = (bf16[80,3584]{1,0:T(8,128)(2,1)S(1)}, bf16[80,3584]{1,0:T(8,128)(2,1)S(1)}, u32[]{:S(2)}, u32[]{:S(2)}) collective-permute-start(bf16[80,3584]{1,0:T(8,128)(2,1)S(1)} %collective-permute-done.10.refs_0_), channel_id=1, source_target_pairs={{0,2},{1,3},{2,0},{3,1},{4,6},{5,7},{6,4},{7,5},{8,10},{9,11},{10,... | collective-permute-start | bytes 1720328 | tf_op jit(solution)/shard_map/chip_2/ppermute | solution.py:37
  62.3 15.9 %collective-permute-start.12 = (bf16[80,3584]{1,0:T(8,128)(2,1)S(1)}, bf16[80,3584]{1,0:T(8,128)(2,1)S(1)}, u32[]{:S(2)}, u32[]{:S(2)}) collective-permute-start(bf16[80,3584]{1,0:T(8,128)(2,1)S(1)} %collective-permute-done.9.refs_0_), channel_id=1, source_target_pairs={{0,2},{1,3},{2,0},{3,1},{4,6},{5,7},{6,4},{7,5},{8,10},{9,11},{10,... | collective-permute-start | bytes 1720328 | tf_op jit(solution)/shard_map/chip_1/ppermute | solution.py:37
  63.7 26.7 %collective-permute-start.7 = (bf16[80,3584]{1,0:T(8,128)(2,1)S(1)}, bf16[80,3584]{1,0:T(8,128)(2,1)S(1)}, u32[]{:S(2)}, u32[]{:S(2)}) collective-permute-start(bf16[80,3584]{1,0:T(8,128)(2,1)S(1)} %get-tuple-element.32), channel_id=1, source_target_pairs={{0,2},{1,3},{2,0},{3,1},{4,6},{5,7},{6,4},{7,5},{8,10},{9,11},{10,... | collective-permute-start | bytes 1720328 | tf_op jit(solution)/shard_map/chip_back_0/ppermute | solution.py:37
  71.4 31.3 %collective-permute-start.18 = (bf16[80,3584]{1,0:T(8,128)(2,1)S(1)}, bf16[80,3584]{1,0:T(8,128)(2,1)S(1)}, u32[]{:S(2)}, u32[]{:S(2)}) collective-permute-start(bf16[80,3584]{1,0:T(8,128)(2,1)S(1)} %collective-permute-done.17.refs_0_), channel_id=1, source_target_pairs={{0,2},{1,3},{2,0},{3,1},{4,6},{5,7},{6,4},{7,5},{8,10},{9,11},{10,... | collective-permute-start | bytes 1720328 | tf_op jit(solution)/shard_map/chip_3/ppermute | solution.py:37
  73.0 42.0 %collective-permute-start.15 = (bf16[80,3584]{1,0:T(8,128)(2,1)S(1)}, bf16[80,3584]{1,0:T(8,128)(2,1)S(1)}, u32[]{:S(2)}, u32[]{:S(2)}) collective-permute-start(bf16[80,3584]{1,0:T(8,128)(2,1)S(1)} %get-tuple-element.41), channel_id=1, source_target_pairs={{0,2},{1,3},{2,0},{3,1},{4,6},{5,7},{6,4},{7,5},{8,10},{9,11},{10,... | collective-permute-start | bytes 1720328 | tf_op jit(solution)/shard_map/chip_back_2/ppermute | solution.py:37
  85.2 41.0 %collective-permute-start.13 = (bf16[80,3584]{1,0:T(8,128)(2,1)S(1)}, bf16[80,3584]{1,0:T(8,128)(2,1)S(1)}, u32[]{:S(2)}, u32[]{:S(2)}) collective-permute-start(bf16[80,3584]{1,0:T(8,128)(2,1)S(1)} %get-tuple-element.40), channel_id=1, source_target_pairs={{0,2},{1,3},{2,0},{3,1},{4,6},{5,7},{6,4},{7,5},{8,10},{9,11},{10,... | collective-permute-start | bytes 1720328 | tf_op jit(solution)/shard_map/chip_back_1/ppermute | solution.py:37
  90.6 43.2 %collective-permute-start.8 = (bf16[80,3584]{1,0:T(8,128)(2,1)S(1)}, bf16[80,3584]{1,0:T(8,128)(2,1)S(1)}, u32[]{:S(2)}, u32[]{:S(2)}) collective-permute-start(bf16[80,3584]{1,0:T(8,128)(2,1)S(1)} %add_convert_fusion.3), channel_id=1, source_target_pairs={{0,16},{1,17},{2,18},{3,19},{4,20},{5,21},{6,22},{7,23},{8,24},{9,... | collective-permute-start | bytes 1720328 | tf_op jit(solution)/shard_map/plane_back_0/ppermute | solution.py:47
  109.8 22.6 %collective-permute-start.19 = (bf16[80,3584]{1,0:T(8,128)(2,1)S(1)}, bf16[80,3584]{1,0:T(8,128)(2,1)S(1)}, u32[]{:S(2)}, u32[]{:S(2)}) collective-permute-start(bf16[80,3584]{1,0:T(8,128)(2,1)S(1)} %get-tuple-element.46), channel_id=1, source_target_pairs={{0,2},{1,3},{2,0},{3,1},{4,6},{5,7},{6,4},{7,5},{8,10},{9,11},{10,... | collective-permute-start | bytes 1720328 | tf_op jit(solution)/shard_map/chip_back_3/ppermute | solution.py:37
  115.2 18.6 %collective-permute-start.16 = (bf16[80,3584]{1,0:T(8,128)(2,1)S(1)}, bf16[80,3584]{1,0:T(8,128)(2,1)S(1)}, u32[]{:S(2)}, u32[]{:S(2)}) collective-permute-start(bf16[80,3584]{1,0:T(8,128)(2,1)S(1)} %add_convert_fusion.1), channel_id=1, source_target_pairs={{0,24},{1,25},{2,26},{3,27},{4,28},{5,29},{6,30},{7,31},{8,16},{9,... | collective-permute-start | bytes 1720328 | tf_op jit(solution)/shard_map/plane_back_2/ppermute | solution.py:47
  126.3 16.1 %collective-permute-start.14 = (bf16[80,3584]{1,0:T(8,128)(2,1)S(1)}, bf16[80,3584]{1,0:T(8,128)(2,1)S(1)}, u32[]{:S(2)}, u32[]{:S(2)}) collective-permute-start(bf16[80,3584]{1,0:T(8,128)(2,1)S(1)} %add_convert_fusion.2), channel_id=1, source_target_pairs={{0,20},{1,21},{2,22},{3,23},{4,16},{5,17},{6,18},{7,19},{8,28},{9,... | collective-permute-start | bytes 1720328 | tf_op jit(solution)/shard_map/plane_back_1/ppermute | solution.py:47
  132.5 27.3 %collective-permute-start.20 = (bf16[80,3584]{1,0:T(8,128)(2,1)S(1)}, bf16[80,3584]{1,0:T(8,128)(2,1)S(1)}, u32[]{:S(2)}, u32[]{:S(2)}) collective-permute-start(bf16[80,3584]{1,0:T(8,128)(2,1)S(1)} %add_convert_fusion), channel_id=1, source_target_pairs={{0,28},{1,29},{2,30},{3,31},{4,24},{5,25},{6,26},{7,27},{8,20},{9,... | collective-permute-start | bytes 1720328 | tf_op jit(solution)/shard_map/plane_back_3/ppermute | solution.py:47

commit v3 on v2

--- a/solution.py
+++ b/solution.py
@@ -9,14 +9,15 @@
 
 SPLIT = 4
 MIB = 1 << 20
+IDS_AT = 1
 
 
 TIES = {
-    ("plane", 3): [("plane", 2), ("pieces", 0)],
-    ("chip", 2): [("pieces", 0)],
-    ("chip", 1): [("pieces", 0)],
+    ("plane", 3): [("plane", 2)],
+    ("chip", 1): [("chip_back", 0), ("pieces", 0), ("plane_back", 0)],
     ("chip", 3): [("pieces", 2)],
-    ("pieces", 1): [("pieces", 2)],
+    ("chip_back", 1): [("plane_back", 2)],
+    ("chip_back", 0): [("chip", 2)],
 }
 
 
@@ -115,7 +116,7 @@
             ],
         ),
         out_shape=[jax.ShapeDtypeStruct((count, width), jnp.bfloat16) for _, _, count in units],
-        compiler_params=pltpu.CompilerParams(vmem_limit_bytes=16 * MIB),
+        compiler_params=pltpu.CompilerParams(vmem_limit_bytes=58 * MIB),
         cost_estimate=pl.CostEstimate(
             flops=1000, bytes_accessed=1000, transcendentals=0
         ),
@@ -174,7 +175,7 @@
         for j in range(2):
             copies.append(
                 pltpu.make_async_copy(
-                    ref.at[source_ref[n // 2, j], pl.ds(first, count)],
+                    ref.at[source_ref[j], pl.ds(first, count)],
                     here.at[n, pl.ds(j * count, count)],
                     sem.at[n, j],
                 )
@@ -266,35 +267,32 @@
             k, first, _ = units[i]
             given = [step(name, i) for name in GIVEN[kind]] if kind != "plane" else [outgoing[i]]
             ties = [first_of(step(*t)) for t in TIES.get((kind, i), ()) if t[1] < len(units)]
-            if ties:
+            mine = own
+            if kind == "pieces":
+                if i == IDS_AT:
+                    ties.append(ids_after)
+                if ties:
+                    mine = after(own, *ties)
+            elif ties:
                 given[0] = after(given[0], *ties)
-            if (kind, i) == ("pieces", 0):
-                given[0] = after(given[0], ids_after)
             with jax.named_scope(f"{kind}_{i}"):
-                values[kind, i] = work(kind, k, first, given)
+                values[kind, i] = work(kind, k, first, given, mine)
         return values[kind, i]
 
-    def work(kind, k, first, given):
+    def work(kind, k, first, given, mine):
         if kind == "plane":
             return exchange(given[0], k * SPLIT) if k else given[0]
         if kind == "chip":
             return exchange(given[0], 2)
         if kind == "pieces":
-            source = ((own ^ k) * SPLIT + (seat ^ jnp.array([0, 2], jnp.int32))).astype(jnp.int32)
-            return pieces(first, jnp.stack([source, source // 2]), given, saved, weights)
+            source = ((mine ^ k) * SPLIT + (seat ^ jnp.array([0, 2], jnp.int32))).astype(jnp.int32)
+            return pieces(first, source, given, saved, weights)
         if kind == "chip_back":
             return exchange(given[0][1], 2)
         return to_section_before(added(given[0][0], given[1]), k * SPLIT)
 
-    with jax.named_scope("ids"):
-        ids_after = to_section_before(after(ids, outgoing[0]), 0)
-    other_core = [
-        lax.dynamic_index_in_dim(
-            v.reshape(experts * SPLIT // 2, 2, *v.shape[1:]), 1 - seat % 2, 1, keepdims=False
-        )
-        for v in (after(gate_saved, outgoing[0]), after(up_saved, outgoing[0]))
-    ]
-    saved = [gate_saved, up_saved] + [exchange(v, 1) for v in other_core]
+    ids_after = to_section_before(ids, 0)
+    saved = [gate_saved, up_saved, exchange(gate_saved, 1), exchange(up_saved, 1)]
     returned = [step("plane_back", i) for i in range(len(units))]
     return combine(own, ids_after, returned, cap, experts, units)[None]
 

time: 163 us -> 157 us (0.963)
  waiting for transfers between devices: 94 us -> 88.4 us
  local copies, waits for them, and re-layouts: 11.3 us -> 8.55 us
    ppermute x5, starting transfers between devices: 8.69 us -> 13.2 us  [to_section_before(): return lax.ppermute(value, ('section', 'ep'), pairs)]
    ppermute x5, waiting for transfers between devices: 28 us -> 24.8 us  [to_section_before(): return lax.ppermute(value, ('section', 'ep'), pairs)]
    ppermute x16, starting transfers between devices: 14.9 us -> 12.1 us  [exchange(): return lax.ppermute(value, 'ep', [(i, i ^ mask) for i in range(count)])]
    pallas_call x1, Pallas kernels: 1.8 us -> 4.34 us  [dispatch(): pl.pallas_call(functools.partial(dispatch_kernel, cap, experts, units), g...]
    ppermute x16, waiting for transfers between devices: 66 us -> 63.6 us  [exchange(): return lax.ppermute(value, 'ep', [(i, i ^ mask) for i in range(count)])]
    squeeze x2 -> x0, local copies, waits for them, and re-layouts: 1.99 us -> none  [local(): lax.dynamic_index_in_dim(v.reshape(experts * SPLIT // 2, 2, *v.shape[1:])...]
    pallas_call x4, Pallas kernels: 28.1 us -> 26.4 us  [pieces(): pl.pallas_call(functools.partial(pieces_kernel, parts, first), in_specs=[...]
    unnamed x26 -> x28, local copies, waits for them, and re-layouts: 9.34 us -> 8.55 us
  transfers between devices with their start and end apart: 21 -> 21, of which waited for: 13 -> 12; matrix products, arithmetic and copies ran while one was open for 2% -> 0% of each run, Pallas kernels for 18% -> 20%
where the time goes in v3:
time: 157 us
  waiting for transfers between devices  88.4 us (56%)
  Pallas kernels  33.7 us (21%)
  starting transfers between devices  25.2 us (16%)
  local copies, waits for them, and re-layouts  8.55 us (5%)
    ppermute x16, waiting for transfers between devices, exchange(): return lax.ppermute(value, 'ep', [(i, i ^ mask) for i in range(count)])  63.6 us
    pallas_call x4, Pallas kernels, pieces(): pl.pallas_call(functools.partial(pieces_kernel, parts, first), in_specs=[...  26.4 us
    ppermute x5, waiting for transfers between devices, to_section_before(): return lax.ppermute(value, ('section', 'ep'), pairs)  24.8 us
    ppermute x5, starting transfers between devices, to_section_before(): return lax.ppermute(value, ('section', 'ep'), pairs)  13.2 us
    ppermute x16, starting transfers between devices, exchange(): return lax.ppermute(value, 'ep', [(i, i ^ mask) for i in range(count)])  12.1 us
    unnamed x28, local copies, waits for them, and re-layouts  8.55 us
    pallas_call x1, Pallas kernels, dispatch(): pl.pallas_call(functools.partial(dispatch_kernel, cap, experts, units), g...  4.34 us
  transfers between devices with their start and end apart: 21, of which 12 were waited for; matrix products, arithmetic and copies ran while one was open for 0% of the time, Pallas kernels for 20%

profile of v3, /device:TPU:16, one launch (start us, length us, event | category | flops | bytes accessed | tf_op | source)
XLA Modules:
  0.0 156.6 jit_solution(427608544826195182)
XLA Ops:
  0.0 0.0 collective-permute-start.4
  0.0 0.5 collective-permute-start.5
  0.5 0.1 collective-permute-start.6
  0.6 4.3 %dispatch.1 = (bf16[80,3584]{1,0:T(8,128)(2,1)}, bf16[80,3584]{1,0:T(8,128)(2,1)}, bf16[80,3584]{1,0:T(8,128)(2,1)}, bf16[80,3584]{1,0:T(8,128)(2,1)}) custom-call(s32[1]{0:T(128)} %bitcast.own_ref, s32[2,128]{1,0:T(2,128)} %bitcast.45, f32[2,128]{1,0:T(2,128)} %bitcast.44, bf16[128,3584]{1,0:T(8,128)(2,1)} %bitcast.43), custom_call_target="tpu_custom_call" | custom-call | flops 1000 | bytes 1000 | tf_op jit(solution)/shard_map/dispatch/pallas_call | solution.py:106
  4.9 1.5 collective-permute-start.1
  6.4 0.3 collective-permute-start.7
  6.7 13.7 %collective-permute-done.1.refs_1_ = bf16[80,3584]{1,0:T(8,128)(2,1)S(1)} collective-permute-done((bf16[80,3584]{1,0:T(8,128)(2,1)}, bf16[80,3584]{1,0:T(8,128)(2,1)S(1)}, u32[]{:S(2)}, u32[]{:S(2)}) %collective-permute-start.1) | collective-permute-done | bytes 573472 | tf_op jit(solution)/shard_map/chip_0/ppermute | solution.py:38
  20.5 0.8 copy-done.10
  21.3 0.0 collective-permute-start.2
  21.3 10.6 %collective-permute-done.7.refs_0_ = bf16[80,3584]{1,0:T(8,128)(2,1)} collective-permute-done((bf16[80,3584]{1,0:T(8,128)(2,1)}, bf16[80,3584]{1,0:T(8,128)(2,1)}, u32[]{:S(2)}, u32[]{:S(2)}) %collective-permute-start.7) | collective-permute-done | bytes 573472 | tf_op jit(solution)/shard_map/plane_2/ppermute | solution.py:38
  31.9 0.0 collective-permute-start.3
  31.9 0.0 collective-permute-done.2.refs_4_
  31.9 0.5 collective-permute-start.8
  32.4 1.9 %collective-permute-done.3.refs_5_ = bf16[16,80,256]{2,1,0:T(8,128)(2,1)} collective-permute-done((bf16[16,80,256]{2,1,0:T(8,128)(2,1)}, bf16[16,80,256]{2,1,0:T(8,128)(2,1)}, u32[]{:S(2)}, u32[]{:S(2)}) %collective-permute-start.3) | collective-permute-done | bytes 655392 | tf_op jit(solution)/shard_map/ppermute | solution.py:38
  34.4 2.6 %collective-permute-start.17 = (bf16[80,3584]{1,0:T(8,128)(2,1)}, bf16[80,3584]{1,0:T(8,128)(2,1)S(1)}, u32[]{:S(2)}, u32[]{:S(2)}) collective-permute-start(bf16[80,3584]{1,0:T(8,128)(2,1)} %get-tuple-element.37), channel_id=1, source_target_pairs={{0,12},{1,13},{2,14},{3,15},{4,8},{5,9},{6,10},{7,11},{8,4},{9,5},... | collective-permute-start | bytes 1720328 | tf_op jit(solution)/shard_map/plane_3/ppermute | solution.py:38
  36.9 0.0 collective-permute-done.4.refs_9_
  37.0 0.0 collective-permute-done.5.refs_10_
  37.0 0.0 collective-permute-done.6.refs_11_
  37.0 0.0 copy-done.6
  37.0 0.0 copy-start
  37.0 1.5 copy-done
  38.5 1.5 copy-done.2
  40.0 1.5 copy-done.4
  41.5 1.1 copy-done.7
  42.6 1.1 copy-done.9
  43.6 1.1 copy-done.11
  44.7 0.0 copy-start.8
  44.7 6.5 %pieces.4 = (bf16[80,3584]{1,0:T(8,128)(2,1)S(1)}, bf16[80,3584]{1,0:T(8,128)(2,1)S(1)}) custom-call(s32[2]{0:T(128)S(1)} %broadcast_add_fusion.3.source_ref, bf16[80,3584]{1,0:T(8,128)(2,1)S(1)} %copy-done.9, bf16[80,3584]{1,0:T(8,128)(2,1)S(1)} %copy-done.11, bf16[16,80,256]{2,1,0:T(8,128)(2,1)S(1)} %bitcast.34, bf16[16,80,256]{2,1,0:T(8,128)(2,1)S(1)} %bitcast.39, ...), custom_call_target="tpu_custom_call" | custom-call | flops 1000 | bytes 1000 | tf_op jit(solution)/shard_map/pieces_0/pieces/pallas_call | solution.py:217
  51.2 0.0 collective-permute-done.8.refs_1_
  51.2 0.6 collective-permute-start.9
  51.8 0.0 copy-done.13
  51.8 2.2 %collective-permute-start.11 = (bf16[80,3584]{1,0:T(8,128)(2,1)S(1)}, bf16[80,3584]{1,0:T(8,128)(2,1)S(1)}, u32[]{:S(2)}, u32[]{:S(2)}) collective-permute-start(bf16[80,3584]{1,0:T(8,128)(2,1)S(1)} %copy-done.13), channel_id=1, source_target_pairs={{0,4},{1,5},{2,6},{3,7},{4,0},{5,1},{6,2},{7,3},{8,12},{9,13},{10,... | collective-permute-start | bytes 1720328 | tf_op jit(solution)/shard_map/plane_1/ppermute | solution.py:38
  54.0 0.0 copy-done.3
  54.0 7.2 %pieces.6 = (bf16[80,3584]{1,0:T(8,128)(2,1)S(1)}, bf16[80,3584]{1,0:T(8,128)(2,1)S(1)}) custom-call(s32[2]{0:T(128)S(1)} %broadcast_add_fusion.1.source_ref, bf16[80,3584]{1,0:T(8,128)(2,1)} %collective-permute-done.7.refs_0_, bf16[80,3584]{1,0:T(8,128)(2,1)} %collective-permute-done.8.refs_1_, bf16[16,80,256]{2,1,0:T(8,128)(2,1)S(1)} %bitcast.35, ...), custom_call_target="tpu_custom_call" | custom-call | flops 1000 | bytes 1000 | tf_op jit(solution)/shard_map/pieces_2/pieces/pallas_call | solution.py:217
  61.3 1.6 %collective-permute-start.13 = (bf16[80,3584]{1,0:T(8,128)(2,1)S(1)}, bf16[80,3584]{1,0:T(8,128)(2,1)S(1)}, u32[]{:S(2)}, u32[]{:S(2)}) collective-permute-start(bf16[80,3584]{1,0:T(8,128)(2,1)S(1)} %get-tuple-element.34), channel_id=1, source_target_pairs={{0,2},{1,3},{2,0},{3,1},{4,6},{5,7},{6,4},{7,5},{8,10},{9,11},{10,... | collective-permute-start | bytes 1720328 | tf_op jit(solution)/shard_map/chip_back_2/ppermute | solution.py:38
  62.9 0.0 collective-permute-done.17.refs_0_
  62.9 0.5 collective-permute-start.18
  63.4 3.8 %collective-permute-done.9 = bf16[80,3584]{1,0:T(8,128)(2,1)S(1)} collective-permute-done((bf16[80,3584]{1,0:T(8,128)(2,1)S(1)}, bf16[80,3584]{1,0:T(8,128)(2,1)S(1)}, u32[]{:S(2)}, u32[]{:S(2)}) %collective-permute-start.9) | collective-permute-done | bytes 573472 | tf_op jit(solution)/shard_map/chip_back_0/ppermute | solution.py:38
  67.1 0.1 add_convert_fusion.3
  67.3 1.6 %collective-permute-start.10 = (bf16[80,3584]{1,0:T(8,128)(2,1)S(1)}, bf16[80,3584]{1,0:T(8,128)(2,1)S(1)}, u32[]{:S(2)}, u32[]{:S(2)}) collective-permute-start(bf16[80,3584]{1,0:T(8,128)(2,1)S(1)} %add_convert_fusion.3), channel_id=1, source_target_pairs={{0,16},{1,17},{2,18},{3,19},{4,20},{5,21},{6,22},{7,23},{8,24},{9,... | collective-permute-start | bytes 1720328 | tf_op jit(solution)/shard_map/plane_back_0/ppermute | solution.py:48
  68.9 10.6 %collective-permute-done.13 = bf16[80,3584]{1,0:T(8,128)(2,1)S(1)} collective-permute-done((bf16[80,3584]{1,0:T(8,128)(2,1)S(1)}, bf16[80,3584]{1,0:T(8,128)(2,1)S(1)}, u32[]{:S(2)}, u32[]{:S(2)}) %collective-permute-start.13) | collective-permute-done | bytes 573472 | tf_op jit(solution)/shard_map/chip_back_2/ppermute | solution.py:38
  79.4 0.1 add_convert_fusion.2
  79.6 5.3 %collective-permute-start.14 = (bf16[80,3584]{1,0:T(8,128)(2,1)S(1)}, bf16[80,3584]{1,0:T(8,128)(2,1)S(1)}, u32[]{:S(2)}, u32[]{:S(2)}) collective-permute-start(bf16[80,3584]{1,0:T(8,128)(2,1)S(1)} %add_convert_fusion.2), channel_id=1, source_target_pairs={{0,24},{1,25},{2,26},{3,27},{4,28},{5,29},{6,30},{7,31},{8,16},{9,... | collective-permute-start | bytes 1720328 | tf_op jit(solution)/shard_map/plane_back_2/ppermute | solution.py:48
  84.9 0.0 collective-permute-done.11.refs_0_
  84.9 0.0 collective-permute-done.10.refs_0_
  84.9 0.5 collective-permute-start.12
  85.4 6.3 %collective-permute-done.18.refs_1_ = bf16[80,3584]{1,0:T(8,128)(2,1)S(1)} collective-permute-done((bf16[80,3584]{1,0:T(8,128)(2,1)S(1)}, bf16[80,3584]{1,0:T(8,128)(2,1)S(1)}, u32[]{:S(2)}, u32[]{:S(2)}) %collective-permute-start.18) | collective-permute-done | bytes 573472 | tf_op jit(solution)/shard_map/chip_3/ppermute | solution.py:38
  91.7 6.3 %pieces.7 = (bf16[80,3584]{1,0:T(8,128)(2,1)S(1)}, bf16[80,3584]{1,0:T(8,128)(2,1)S(1)}) custom-call(s32[2]{0:T(128)S(1)} %broadcast_add_fusion.source_ref, bf16[80,3584]{1,0:T(8,128)(2,1)S(1)} %collective-permute-done.17.refs_0_, bf16[80,3584]{1,0:T(8,128)(2,1)S(1)} %collective-permute-done.18.refs_1_, bf16[16,80,256]{2,1,0:T(8,128)(2,1)S(1)} %bitcast.36, ...), custom_call_target="tpu_custom_call" | custom-call | flops 1000 | bytes 1000 | tf_op jit(solution)/shard_map/pieces_3/pieces/pallas_call | solution.py:217
  98.1 0.6 collective-permute-start.19
  98.6 1.5 collective-permute-start
  100.2 2.0 %collective-permute-done.ids_ref = s32[2,128]{1,0:T(2,128)S(1)} collective-permute-done((s32[2,128]{1,0:T(2,128)S(1)}, s32[2,128]{1,0:T(2,128)S(1)}, u32[]{:S(2)}, u32[]{:S(2)}) %collective-permute-start) | collective-permute-done | bytes 1056 | tf_op jit(solution)/shard_map/ppermute | solution.py:48
  102.2 1.8 %collective-permute-done.12.refs_1_ = bf16[80,3584]{1,0:T(8,128)(2,1)S(1)} collective-permute-done((bf16[80,3584]{1,0:T(8,128)(2,1)S(1)}, bf16[80,3584]{1,0:T(8,128)(2,1)S(1)}, u32[]{:S(2)}, u32[]{:S(2)}) %collective-permute-start.12) | collective-permute-done | bytes 573472 | tf_op jit(solution)/shard_map/chip_1/ppermute | solution.py:38
  104.0 6.3 %pieces.5 = (bf16[80,3584]{1,0:T(8,128)(2,1)S(1)}, bf16[80,3584]{1,0:T(8,128)(2,1)S(1)}) custom-call(s32[2]{0:T(128)S(1)} %broadcast_add_fusion.2.source_ref, bf16[80,3584]{1,0:T(8,128)(2,1)S(1)} %collective-permute-done.11.refs_0_, bf16[80,3584]{1,0:T(8,128)(2,1)S(1)} %collective-permute-done.12.refs_1_, bf16[16,80,256]{2,1,0:T(8,128)(2,1)S(1)} %bitcast.37, ...), custom_call_target="tpu_custom_call" | custom-call | flops 1000 | bytes 1000 | tf_op jit(solution)/shard_map/pieces_1/pieces/pallas_call | solution.py:217
  110.4 0.0 collective-permute-done.14.refs_2_
  110.4 0.6 collective-permute-start.15
  110.9 5.4 %collective-permute-done.19 = bf16[80,3584]{1,0:T(8,128)(2,1)S(1)} collective-permute-done((bf16[80,3584]{1,0:T(8,128)(2,1)S(1)}, bf16[80,3584]{1,0:T(8,128)(2,1)S(1)}, u32[]{:S(2)}, u32[]{:S(2)}) %collective-permute-start.19) | collective-permute-done | bytes 573472 | tf_op jit(solution)/shard_map/chip_back_3/ppermute | solution.py:38
  116.3 0.1 add_convert_fusion
  116.4 1.5 collective-permute-start.20
  117.9 9.5 %collective-permute-done.15 = bf16[80,3584]{1,0:T(8,128)(2,1)S(1)} collective-permute-done((bf16[80,3584]{1,0:T(8,128)(2,1)S(1)}, bf16[80,3584]{1,0:T(8,128)(2,1)S(1)}, u32[]{:S(2)}, u32[]{:S(2)}) %collective-permute-start.15) | collective-permute-done | bytes 573472 | tf_op jit(solution)/shard_map/chip_back_1/ppermute | solution.py:38
  127.4 0.1 add_convert_fusion.1
  127.6 3.3 %collective-permute-start.16 = (bf16[80,3584]{1,0:T(8,128)(2,1)S(1)}, bf16[80,3584]{1,0:T(8,128)(2,1)S(1)}, u32[]{:S(2)}, u32[]{:S(2)}) collective-permute-start(bf16[80,3584]{1,0:T(8,128)(2,1)S(1)} %add_convert_fusion.1), channel_id=1, source_target_pairs={{0,20},{1,21},{2,22},{3,23},{4,16},{5,17},{6,18},{7,19},{8,28},{9,... | collective-permute-start | bytes 1720328 | tf_op jit(solution)/shard_map/plane_back_1/ppermute | solution.py:48
  130.9 20.2 %collective-permute-done.20.refs_3_ = bf16[80,3584]{1,0:T(8,128)(2,1)S(1)} collective-permute-done((bf16[80,3584]{1,0:T(8,128)(2,1)S(1)}, bf16[80,3584]{1,0:T(8,128)(2,1)S(1)}, u32[]{:S(2)}, u32[]{:S(2)}) %collective-permute-start.20) | collective-permute-done | bytes 573472 | tf_op jit(solution)/shard_map/plane_back_3/ppermute | solution.py:48
  151.0 2.6 %collective-permute-done.16.refs_1_ = bf16[80,3584]{1,0:T(8,128)(2,1)S(1)} collective-permute-done((bf16[80,3584]{1,0:T(8,128)(2,1)S(1)}, bf16[80,3584]{1,0:T(8,128)(2,1)S(1)}, u32[]{:S(2)}, u32[]{:S(2)}) %collective-permute-start.16) | collective-permute-done | bytes 573472 | tf_op jit(solution)/shard_map/plane_back_1/ppermute | solution.py:48
  153.6 3.0 %combine.1 = bf16[128,3584]{1,0:T(8,128)(2,1)} custom-call(s32[1]{0:T(128)} %bitcast.own_ref, s32[2,128]{1,0:T(2,128)S(1)} %collective-permute-done.ids_ref, bf16[80,3584]{1,0:T(8,128)(2,1)S(1)} %collective-permute-done.10.refs_0_, bf16[80,3584]{1,0:T(8,128)(2,1)S(1)} %collective-permute-done.16.refs_1_, ...), custom_call_target="tpu_custom_call" | custom-call | flops 1000 | bytes 1000 | tf_op jit(solution)/shard_map/combine/pallas_call | solution.py:149
  (20 shorter events, 0.0 us)
Async XLA Ops:
  0.0 37.0 %copy-start.6 = (bf16[1,1,16,80,256]{4,3,2,1,0:T(8,128)(2,1)S(1)}, bf16[1,1,16,80,256]{4,3,2,1,0:T(8,128)(2,1)}, u32[]{:S(2)}) copy-start(bf16[1,1,16,80,256]{4,3,2,1,0:T(8,128)(2,1)} %param.15) | copy-start | bytes 1966084
  0.0 36.9 %collective-permute-start.4 = (bf16[3584,256]{1,0:T(8,128)(2,1)}, bf16[3584,256]{1,0:T(8,128)(2,1)S(1)}, u32[]{:S(2)}, u32[]{:S(2)}) collective-permute-start(bf16[3584,256]{1,0:T(8,128)(2,1)} %bitcast.18), channel_id=1, source_target_pairs={{0,1},{1,0},{2,3},{3,2},{4,5},{5,4},{6,7},{7,6},{8,9},{9,8},{10,11... | collective-permute-start | bytes 5505032 | tf_op jit(solution)/shard_map/ppermute | solution.py:38
  0.0 36.9 %collective-permute-start.5 = (bf16[3584,256]{1,0:T(8,128)(2,1)}, bf16[3584,256]{1,0:T(8,128)(2,1)}, u32[]{:S(2)}, u32[]{:S(2)}) collective-permute-start(bf16[3584,256]{1,0:T(8,128)(2,1)} %bitcast.23), channel_id=1, source_target_pairs={{0,1},{1,0},{2,3},{3,2},{4,5},{5,4},{6,7},{7,6},{8,9},{9,8},{10,11... | collective-permute-start | bytes 5505032 | tf_op jit(solution)/shard_map/ppermute | solution.py:38
  0.5 36.4 %collective-permute-start.6 = (bf16[256,3584]{1,0:T(8,128)(2,1)}, bf16[256,3584]{1,0:T(8,128)(2,1)}, u32[]{:S(2)}, u32[]{:S(2)}) collective-permute-start(bf16[256,3584]{1,0:T(8,128)(2,1)} %bitcast.28), channel_id=1, source_target_pairs={{0,1},{1,0},{2,3},{3,2},{4,5},{5,4},{6,7},{7,6},{8,9},{9,8},{10,11... | collective-permute-start | bytes 5505032 | tf_op jit(solution)/shard_map/ppermute | solution.py:38
  4.9 15.5 %collective-permute-start.1 = (bf16[80,3584]{1,0:T(8,128)(2,1)}, bf16[80,3584]{1,0:T(8,128)(2,1)S(1)}, u32[]{:S(2)}, u32[]{:S(2)}) collective-permute-start(bf16[80,3584]{1,0:T(8,128)(2,1)} %get-tuple-element.23.refs_0_), channel_id=1, source_target_pairs={{0,2},{1,3},{2,0},{3,1},{4,6},{5,7},{6,4},{7,5},{8,10},{9,11},{10,... | collective-permute-start | bytes 1720328 | tf_op jit(solution)/shard_map/chip_0/ppermute | solution.py:38
  6.4 25.5 %collective-permute-start.7 = (bf16[80,3584]{1,0:T(8,128)(2,1)}, bf16[80,3584]{1,0:T(8,128)(2,1)}, u32[]{:S(2)}, u32[]{:S(2)}) collective-permute-start(bf16[80,3584]{1,0:T(8,128)(2,1)} %get-tuple-element.26), channel_id=1, source_target_pairs={{0,8},{1,9},{2,10},{3,11},{4,12},{5,13},{6,14},{7,15},{8,0},{9,1},... | collective-permute-start | bytes 1720328 | tf_op jit(solution)/shard_map/plane_2/ppermute | solution.py:38
  20.5 0.8 copy-start.10
  21.3 10.6 %collective-permute-start.2 = (bf16[16,80,256]{2,1,0:T(8,128)(2,1)}, bf16[16,80,256]{2,1,0:T(8,128)(2,1)S(1)}, u32[]{:S(2)}, u32[]{:S(2)}) collective-permute-start(bf16[16,80,256]{2,1,0:T(8,128)(2,1)} %bitcast.33), channel_id=1, source_target_pairs={{0,1},{1,0},{2,3},{3,2},{4,5},{5,4},{6,7},{7,6},{8,9},{9,8},{10,11... | collective-permute-start | bytes 1966088 | tf_op jit(solution)/shard_map/ppermute | solution.py:38
  31.9 2.4 %collective-permute-start.3 = (bf16[16,80,256]{2,1,0:T(8,128)(2,1)}, bf16[16,80,256]{2,1,0:T(8,128)(2,1)}, u32[]{:S(2)}, u32[]{:S(2)}) collective-permute-start(bf16[16,80,256]{2,1,0:T(8,128)(2,1)} %bitcast.38), channel_id=1, source_target_pairs={{0,1},{1,0},{2,3},{3,2},{4,5},{5,4},{6,7},{7,6},{8,9},{9,8},{10,11... | collective-permute-start | bytes 1966088 | tf_op jit(solution)/shard_map/ppermute | solution.py:38
  31.9 19.3 %collective-permute-start.8 = (bf16[80,3584]{1,0:T(8,128)(2,1)}, bf16[80,3584]{1,0:T(8,128)(2,1)}, u32[]{:S(2)}, u32[]{:S(2)}) collective-permute-start(bf16[80,3584]{1,0:T(8,128)(2,1)} %collective-permute-done.7.refs_0_), channel_id=1, source_target_pairs={{0,2},{1,3},{2,0},{3,1},{4,6},{5,7},{6,4},{7,5},{8,10},{9,11},{10,... | collective-permute-start | bytes 1720328 | tf_op jit(solution)/shard_map/chip_2/ppermute | solution.py:38
  34.4 28.6 %collective-permute-start.17 = (bf16[80,3584]{1,0:T(8,128)(2,1)}, bf16[80,3584]{1,0:T(8,128)(2,1)S(1)}, u32[]{:S(2)}, u32[]{:S(2)}) collective-permute-start(bf16[80,3584]{1,0:T(8,128)(2,1)} %get-tuple-element.37), channel_id=1, source_target_pairs={{0,12},{1,13},{2,14},{3,15},{4,8},{5,9},{6,10},{7,11},{8,4},{9,5},... | collective-permute-start | bytes 1720328 | tf_op jit(solution)/shard_map/plane_3/ppermute | solution.py:38
  37.0 1.5 copy-start
  38.5 1.5 copy-start.2
  40.0 1.5 copy-start.4
  41.5 1.1 copy-start.7
  42.6 1.1 copy-start.9
  43.6 1.1 copy-start.11
  44.7 7.1 %copy-start.13 = (bf16[80,3584]{1,0:T(8,128)(2,1)S(1)}, bf16[80,3584]{1,0:T(8,128)(2,1)}, u32[]{:S(2)}) copy-start(bf16[80,3584]{1,0:T(8,128)(2,1)} %get-tuple-element.29) | copy-start | bytes 1720324
  44.7 9.3 %copy-start.1 = (bf16[1,1,3584,256]{3,2,1,0:T(8,128)(2,1)S(1)}, bf16[1,1,3584,256]{3,2,1,0:T(8,128)(2,1)}, u32[]{:S(2)}) copy-start(bf16[1,1,3584,256]{3,2,1,0:T(8,128)(2,1)} %param.17) | copy-start | bytes 5505028
  44.7 9.3 %copy-start.3 = (bf16[1,1,3584,256]{3,2,1,0:T(8,128)(2,1)S(1)}, bf16[1,1,3584,256]{3,2,1,0:T(8,128)(2,1)}, u32[]{:S(2)}) copy-start(bf16[1,1,3584,256]{3,2,1,0:T(8,128)(2,1)} %param.18) | copy-start | bytes 5505028
  44.7 9.3 %copy-start.5 = (bf16[1,1,256,3584]{3,2,1,0:T(8,128)(2,1)S(1)}, bf16[1,1,256,3584]{3,2,1,0:T(8,128)(2,1)}, u32[]{:S(2)}) copy-start(bf16[1,1,256,3584]{3,2,1,0:T(8,128)(2,1)} %param.19) | copy-start | bytes 5505028
  44.7 9.3 %copy-start.8 = (bf16[1,1,16,80,256]{4,3,2,1,0:T(8,128)(2,1)S(1)}, bf16[1,1,16,80,256]{4,3,2,1,0:T(8,128)(2,1)}, u32[]{:S(2)}) copy-start(bf16[1,1,16,80,256]{4,3,2,1,0:T(8,128)(2,1)} %param.16) | copy-start | bytes 1966084
  51.2 15.9 %collective-permute-start.9 = (bf16[80,3584]{1,0:T(8,128)(2,1)S(1)}, bf16[80,3584]{1,0:T(8,128)(2,1)S(1)}, u32[]{:S(2)}, u32[]{:S(2)}) collective-permute-start(bf16[80,3584]{1,0:T(8,128)(2,1)S(1)} %get-tuple-element.27), channel_id=1, source_target_pairs={{0,2},{1,3},{2,0},{3,1},{4,6},{5,7},{6,4},{7,5},{8,10},{9,11},{10,... | collective-permute-start | bytes 1720328 | tf_op jit(solution)/shard_map/chip_back_0/ppermute | solution.py:38
  51.8 33.1 %collective-permute-start.11 = (bf16[80,3584]{1,0:T(8,128)(2,1)S(1)}, bf16[80,3584]{1,0:T(8,128)(2,1)S(1)}, u32[]{:S(2)}, u32[]{:S(2)}) collective-permute-start(bf16[80,3584]{1,0:T(8,128)(2,1)S(1)} %copy-done.13), channel_id=1, source_target_pairs={{0,4},{1,5},{2,6},{3,7},{4,0},{5,1},{6,2},{7,3},{8,12},{9,13},{10,... | collective-permute-start | bytes 1720328 | tf_op jit(solution)/shard_map/plane_1/ppermute | solution.py:38
  61.3 18.2 %collective-permute-start.13 = (bf16[80,3584]{1,0:T(8,128)(2,1)S(1)}, bf16[80,3584]{1,0:T(8,128)(2,1)S(1)}, u32[]{:S(2)}, u32[]{:S(2)}) collective-permute-start(bf16[80,3584]{1,0:T(8,128)(2,1)S(1)} %get-tuple-element.34), channel_id=1, source_target_pairs={{0,2},{1,3},{2,0},{3,1},{4,6},{5,7},{6,4},{7,5},{8,10},{9,11},{10,... | collective-permute-start | bytes 1720328 | tf_op jit(solution)/shard_map/chip_back_2/ppermute | solution.py:38
  62.9 28.8 %collective-permute-start.18 = (bf16[80,3584]{1,0:T(8,128)(2,1)S(1)}, bf16[80,3584]{1,0:T(8,128)(2,1)S(1)}, u32[]{:S(2)}, u32[]{:S(2)}) collective-permute-start(bf16[80,3584]{1,0:T(8,128)(2,1)S(1)} %collective-permute-done.17.refs_0_), channel_id=1, source_target_pairs={{0,2},{1,3},{2,0},{3,1},{4,6},{5,7},{6,4},{7,5},{8,10},{9,11},{10,... | collective-permute-start | bytes 1720328 | tf_op jit(solution)/shard_map/chip_3/ppermute | solution.py:38
  67.3 17.6 %collective-permute-start.10 = (bf16[80,3584]{1,0:T(8,128)(2,1)S(1)}, bf16[80,3584]{1,0:T(8,128)(2,1)S(1)}, u32[]{:S(2)}, u32[]{:S(2)}) collective-permute-start(bf16[80,3584]{1,0:T(8,128)(2,1)S(1)} %add_convert_fusion.3), channel_id=1, source_target_pairs={{0,16},{1,17},{2,18},{3,19},{4,20},{5,21},{6,22},{7,23},{8,24},{9,... | collective-permute-start | bytes 1720328 | tf_op jit(solution)/shard_map/plane_back_0/ppermute | solution.py:48
  79.6 30.8 %collective-permute-start.14 = (bf16[80,3584]{1,0:T(8,128)(2,1)S(1)}, bf16[80,3584]{1,0:T(8,128)(2,1)S(1)}, u32[]{:S(2)}, u32[]{:S(2)}) collective-permute-start(bf16[80,3584]{1,0:T(8,128)(2,1)S(1)} %add_convert_fusion.2), channel_id=1, source_target_pairs={{0,24},{1,25},{2,26},{3,27},{4,28},{5,29},{6,30},{7,31},{8,16},{9,... | collective-permute-start | bytes 1720328 | tf_op jit(solution)/shard_map/plane_back_2/ppermute | solution.py:48
  84.9 19.1 %collective-permute-start.12 = (bf16[80,3584]{1,0:T(8,128)(2,1)S(1)}, bf16[80,3584]{1,0:T(8,128)(2,1)S(1)}, u32[]{:S(2)}, u32[]{:S(2)}) collective-permute-start(bf16[80,3584]{1,0:T(8,128)(2,1)S(1)} %collective-permute-done.11.refs_0_), channel_id=1, source_target_pairs={{0,2},{1,3},{2,0},{3,1},{4,6},{5,7},{6,4},{7,5},{8,10},{9,11},{10,... | collective-permute-start | bytes 1720328 | tf_op jit(solution)/shard_map/chip_1/ppermute | solution.py:38
  85.4 13.2 %copy-start.12 = (s32[1,128,2]{1,2,0:T(2,128)S(1)}, s32[1,128,2]{1,2,0:T(2,128)}, u32[]{:S(2)}) copy-start(s32[1,128,2]{1,2,0:T(2,128)} %param.13) | copy-start | bytes 3076
  98.1 18.2 %collective-permute-start.19 = (bf16[80,3584]{1,0:T(8,128)(2,1)S(1)}, bf16[80,3584]{1,0:T(8,128)(2,1)S(1)}, u32[]{:S(2)}, u32[]{:S(2)}) collective-permute-start(bf16[80,3584]{1,0:T(8,128)(2,1)S(1)} %get-tuple-element.40), channel_id=1, source_target_pairs={{0,2},{1,3},{2,0},{3,1},{4,6},{5,7},{6,4},{7,5},{8,10},{9,11},{10,... | collective-permute-start | bytes 1720328 | tf_op jit(solution)/shard_map/chip_back_3/ppermute | solution.py:38
  98.6 3.6 %collective-permute-start = (s32[2,128]{1,0:T(2,128)S(1)}, s32[2,128]{1,0:T(2,128)S(1)}, u32[]{:S(2)}, u32[]{:S(2)}) collective-permute-start(s32[2,128]{1,0:T(2,128)S(1)} %bitcast.46), channel_id=1, source_target_pairs={{0,16},{1,17},{2,18},{3,19},{4,20},{5,21},{6,22},{7,23},{8,24},{9,... | collective-permute-start | bytes 3080 | tf_op jit(solution)/shard_map/ppermute | solution.py:48
  110.4 17.1 %collective-permute-start.15 = (bf16[80,3584]{1,0:T(8,128)(2,1)S(1)}, bf16[80,3584]{1,0:T(8,128)(2,1)S(1)}, u32[]{:S(2)}, u32[]{:S(2)}) collective-permute-start(bf16[80,3584]{1,0:T(8,128)(2,1)S(1)} %get-tuple-element.35), channel_id=1, source_target_pairs={{0,2},{1,3},{2,0},{3,1},{4,6},{5,7},{6,4},{7,5},{8,10},{9,11},{10,... | collective-permute-start | bytes 1720328 | tf_op jit(solution)/shard_map/chip_back_1/ppermute | solution.py:38
  116.4 34.6 %collective-permute-start.20 = (bf16[80,3584]{1,0:T(8,128)(2,1)S(1)}, bf16[80,3584]{1,0:T(8,128)(2,1)S(1)}, u32[]{:S(2)}, u32[]{:S(2)}) collective-permute-start(bf16[80,3584]{1,0:T(8,128)(2,1)S(1)} %add_convert_fusion), channel_id=1, source_target_pairs={{0,28},{1,29},{2,30},{3,31},{4,24},{5,25},{6,26},{7,27},{8,20},{9,... | collective-permute-start | bytes 1720328 | tf_op jit(solution)/shard_map/plane_back_3/ppermute | solution.py:48
  127.6 26.1 %collective-permute-start.16 = (bf16[80,3584]{1,0:T(8,128)(2,1)S(1)}, bf16[80,3584]{1,0:T(8,128)(2,1)S(1)}, u32[]{:S(2)}, u32[]{:S(2)}) collective-permute-start(bf16[80,3584]{1,0:T(8,128)(2,1)S(1)} %add_convert_fusion.1), channel_id=1, source_target_pairs={{0,20},{1,21},{2,22},{3,23},{4,16},{5,17},{6,18},{7,19},{8,28},{9,... | collective-permute-start | bytes 1720328 | tf_op jit(solution)/shard_map/plane_back_1/ppermute | solution.py:48

commit v4 on v3

--- a/solution.py
+++ b/solution.py
@@ -10,27 +10,29 @@
 SPLIT = 4
 MIB = 1 << 20
 IDS_AT = 1
+COSTS = (1000, 1000, 100000000000, 100000000000)
 
 
 TIES = {
-    ("plane", 3): [("plane", 2)],
-    ("chip", 1): [("chip_back", 0), ("pieces", 0), ("plane_back", 0)],
-    ("chip", 3): [("pieces", 2)],
-    ("chip_back", 1): [("plane_back", 2)],
-    ("chip_back", 0): [("chip", 2)],
+    ("plane", 4): [("plane", 3)],
+    ("chip", 1): [("chip_back", 0)],
+    ("chip", 4): [("pieces", 2)],
+    ("chip_back", 1): [("plane_back", 3)],
+    ("chip_back", 2): [("plane_back", 3)],
+    ("chip_back", 0): [("chip", 3)],
+    ("plane_back", 4): [("pieces", 1)],
 }
 
 
 def cut(experts, cap):
-    return [(k, 0, cap) for k in range(experts)]
-
-
-GIVEN = {
-    "chip": ("plane",),
-    "pieces": ("plane", "chip"),
-    "chip_back": ("pieces",),
-    "plane_back": ("pieces", "chip_back"),
-}
+    head = -(-cap // 32) * 16
+    units = []
+    for k in range(experts):
+        if k == 1:
+            units += [(k, 0, head), (k, head, cap - head)]
+        else:
+            units.append((k, 0, cap))
+    return units
 
 
 def exchange(value, mask):
@@ -165,19 +167,25 @@
     )(own, ids, *returned)
 
 
-def pieces_kernel(parts, first, source_ref, *refs):
-    blocks, saved, weights, outs = refs[:2], refs[2:6], refs[6:12], refs[12:14]
-    here, sem = refs[14:]
-    count, width = blocks[0].shape
+def pieces_kernel(parts, spans, source_ref, *refs):
+    blocks, refs = refs[: 2 * len(spans)], refs[2 * len(spans) :]
+    saved, weights, refs = refs[:4], refs[4:10], refs[10:]
+    outs, (here, sem) = refs[:-2], refs[-2:]
+    width = blocks[0].shape[1]
     tile = width // parts
+    places, at = [], 0
+    for j in range(2):
+        for first, count in spans:
+            places.append((j, first, count, at))
+            at += count
     copies = []
     for n, ref in enumerate(saved):
-        for j in range(2):
+        for i, (j, first, count, at) in enumerate(places):
             copies.append(
                 pltpu.make_async_copy(
                     ref.at[source_ref[j], pl.ds(first, count)],
-                    here.at[n, pl.ds(j * count, count)],
-                    sem.at[n, j],
+                    here.at[n, pl.ds(at, count)],
+                    sem.at[n, i],
                 )
             )
     for copy in copies:
@@ -198,33 +206,39 @@
         grads.append((totals[n] * u * s * (1.0 + g * (1.0 - s))).astype(jnp.bfloat16))
         grads.append((totals[n] * g * s).astype(jnp.bfloat16))
     for i in range(parts):
-        at = pl.ds(i * tile, tile)
+        columns = pl.ds(i * tile, tile)
         part = None
         for grad, weight in zip(grads, (weights[0], weights[1], weights[3], weights[4])):
-            term = lax.dot_general(grad, weight[at, :], across, preferred_element_type=jnp.float32)
+            term = lax.dot_general(
+                grad, weight[columns, :], across, preferred_element_type=jnp.float32
+            )
             part = term if part is None else part + term
         part = part.astype(jnp.bfloat16)
-        for j in range(2):
-            outs[j][:, at] = part[j * count : (j + 1) * count, :]
-
-
-def pieces(first, source, blocks, saved, weights):
-    count, width = blocks[0].shape
+        for out_ref, (_, _, count, at) in zip(outs, places):
+            out_ref[:, columns] = part[at : at + count, :]
+
+
+def pieces(cost, spans, source, blocks, saved, weights):
+    width = blocks[0].shape[1]
     hidden = weights[2].shape[0]
     parts = width // 512 if width % 512 == 0 else 1
+    rows = sum(block.shape[0] for block in blocks)
     anywhere = pl.BlockSpec(memory_space=pl.ANY)
     near = pl.BlockSpec(memory_space=pltpu.VMEM)
     return pl.pallas_call(
-        functools.partial(pieces_kernel, parts, first),
-        in_specs=[pl.BlockSpec(memory_space=pltpu.SMEM)] + [near] * 2 + [anywhere] * 4 + [near] * 6,
-        out_specs=[near] * 2,
-        out_shape=[jax.ShapeDtypeStruct((count, width), jnp.bfloat16)] * 2,
+        functools.partial(pieces_kernel, parts, spans),
+        in_specs=[pl.BlockSpec(memory_space=pltpu.SMEM)]
+        + [near] * len(blocks)
+        + [anywhere] * 4
+        + [near] * 6,
+        out_specs=[near] * len(blocks),
+        out_shape=[jax.ShapeDtypeStruct(block.shape, jnp.bfloat16) for block in blocks],
         scratch_shapes=[
-            pltpu.VMEM((4, 2 * count, hidden), jnp.bfloat16),
-            pltpu.SemaphoreType.DMA((4, 2)),
+            pltpu.VMEM((4, rows, hidden), jnp.bfloat16),
+            pltpu.SemaphoreType.DMA((4, len(blocks))),
         ],
         compiler_params=pltpu.CompilerParams(vmem_limit_bytes=20 * MIB),
-        cost_estimate=pl.CostEstimate(flops=1000, bytes_accessed=1000, transcendentals=0),
+        cost_estimate=pl.CostEstimate(flops=cost, bytes_accessed=1000, transcendentals=0),
         name="pieces",
     )(source, *blocks, *saved, *weights)
 
@@ -262,34 +276,42 @@
     weights = weights + [exchange(w, 1) for w in weights]
     values = {}
 
+    def parts_of(k):
+        return [j for j, unit in enumerate(units) if unit[0] == k]
+
     def step(kind, i):
         if (kind, i) not in values:
-            k, first, _ = units[i]
-            given = [step(name, i) for name in GIVEN[kind]] if kind != "plane" else [outgoing[i]]
+            if kind == "pieces":
+                given = [step(name, j) for name in ("plane", "chip") for j in parts_of(i)]
+            elif kind == "plane":
+                given = [outgoing[i]]
+            elif kind == "chip":
+                given = [step("plane", i)]
+            else:
+                mine = parts_of(units[i][0])
+                rows = step("pieces", units[i][0])
+                at = mine.index(i)
+                given = [rows[at], rows[len(mine) + at]]
+                given = given[1:] if kind == "chip_back" else [given[0], step("chip_back", i)]
             ties = [first_of(step(*t)) for t in TIES.get((kind, i), ()) if t[1] < len(units)]
-            mine = own
-            if kind == "pieces":
-                if i == IDS_AT:
-                    ties.append(ids_after)
-                if ties:
-                    mine = after(own, *ties)
-            elif ties:
-                given[0] = after(given[0], *ties)
             with jax.named_scope(f"{kind}_{i}"):
-                values[kind, i] = work(kind, k, first, given, mine)
+                values[kind, i] = work(kind, i, given, ties)
         return values[kind, i]
 
-    def work(kind, k, first, given, mine):
+    def work(kind, i, given, ties):
+        if kind == "pieces":
+            ties = ties + [ids_after] * (i == IDS_AT)
+            mine = after(own, *ties) if ties else own
+            source = ((mine ^ i) * SPLIT + (seat ^ jnp.array([0, 2], jnp.int32))).astype(jnp.int32)
+            return pieces(COSTS[i % len(COSTS)], [units[j][1:] for j in parts_of(i)], source, given, saved, weights)
+        if ties:
+            given[0] = after(given[0], *ties)
+        k = units[i][0]
         if kind == "plane":
             return exchange(given[0], k * SPLIT) if k else given[0]
-        if kind == "chip":
+        if kind in ("chip", "chip_back"):
             return exchange(given[0], 2)
-        if kind == "pieces":
-            source = ((mine ^ k) * SPLIT + (seat ^ jnp.array([0, 2], jnp.int32))).astype(jnp.int32)
-            return pieces(first, source, given, saved, weights)
-        if kind == "chip_back":
-            return exchange(given[0][1], 2)
-        return to_section_before(added(given[0][0], given[1]), k * SPLIT)
+        return to_section_before(added(*given), k * SPLIT)
 
     ids_after = to_section_before(ids, 0)
     saved = [gate_saved, up_saved, exchange(gate_saved, 1), exchange(up_saved, 1)]

time: 157 us -> 152 us (0.968)
  waiting for transfers between devices: 88.4 us -> 74.4 us
  starting transfers between devices: 25.2 us -> 32.2 us
    ppermute x5 -> x6, waiting for transfers between devices: 24.8 us -> 17.8 us  [to_section_before(): return lax.ppermute(value, ('section', 'ep'), pairs)]
    ppermute x16 -> x19, waiting for transfers between devices: 63.6 us -> 56.6 us  [exchange(): return lax.ppermute(value, 'ep', [(i, i ^ mask) for i in range(count)])]
    ppermute x5 -> x6, starting transfers between devices: 13.2 us -> 17 us  [to_section_before(): return lax.ppermute(value, ('section', 'ep'), pairs)]
    ppermute x16 -> x19, starting transfers between devices: 12.1 us -> 15.2 us  [exchange(): return lax.ppermute(value, 'ep', [(i, i ^ mask) for i in range(count)])]
    unnamed x28 -> x30, local copies, waits for them, and re-layouts: 8.55 us -> 8.55 us
  transfers between devices with their start and end apart: 21 -> 25, of which waited for: 12 -> 10; matrix products, arithmetic and copies ran while one was open for 0% -> 0% of each run, Pallas kernels for 20% -> 21%
where the time goes in v4:
time: 152 us; the launch traced here: 150 us
  waiting for transfers between devices  74.4 us (49%)
  Pallas kernels  34.5 us (23%)
  starting transfers between devices  32.2 us (21%)
  local copies, waits for them, and re-layouts  8.55 us (6%)
    ppermute x19, waiting for transfers between devices, exchange(): return lax.ppermute(value, 'ep', [(i, i ^ mask) for i in range(count)])  56.6 us
    pallas_call x4, Pallas kernels, pieces(): pl.pallas_call(functools.partial(pieces_kernel, parts, spans), in_specs=[...  27 us
    ppermute x6, waiting for transfers between devices, to_section_before(): return lax.ppermute(value, ('section', 'ep'), pairs)  17.8 us
    ppermute x6, starting transfers between devices, to_section_before(): return lax.ppermute(value, ('section', 'ep'), pairs)  17 us
    ppermute x19, starting transfers between devices, exchange(): return lax.ppermute(value, 'ep', [(i, i ^ mask) for i in range(count)])  15.2 us
    unnamed x30, local copies, waits for them, and re-layouts  8.55 us
    pallas_call x1, Pallas kernels, dispatch(): pl.pallas_call(functools.partial(dispatch_kernel, cap, experts, units), g...  4.33 us
    pallas_call x1, Pallas kernels, combine(): pl.pallas_call(functools.partial(combine_kernel, cap, experts, units), gr...  3.2 us
  transfers between devices with their start and end apart: 25, of which 10 were waited for; matrix products, arithmetic and copies ran while one was open for 0% of the time, Pallas kernels for 21%

profile of v4, /device:TPU:16, one launch (start us, length us, event | category | flops | bytes accessed | tf_op | source)
XLA Modules:
  0.0 150.4 jit_solution(11995317532535955998)
XLA Ops:
  0.0 0.0 collective-permute-start.4
  0.0 0.5 collective-permute-start.5
  0.5 0.1 collective-permute-start.6
  0.6 4.3 %dispatch.1 = (bf16[80,3584]{1,0:T(8,128)(2,1)}, bf16[48,3584]{1,0:T(8,128)(2,1)}, bf16[32,3584]{1,0:T(8,128)(2,1)}, bf16[80,3584]{1,0:T(8,128)(2,1)}, bf16[80,3584]{1,0:T(8,128)(2,1)}) custom-call(s32[1]{0:T(128)} %bitcast.own_ref, s32[2,128]{1,0:T(2,128)} %bitcast.45, f32[2,128]{1,0:T(2,128)} %bitcast.44, bf16[128,3584]{1,0:T(8,128)(2,1)} %bitcast.43), custom_call_target="tpu_custom_call" | custom-call | flops 1000 | bytes 1000 | tf_op jit(solution)/shard_map/dispatch/pallas_call | solution.py:108
  4.9 1.5 collective-permute-start.1
  6.4 0.3 collective-permute-start.7
  6.7 13.7 %collective-permute-done.1.refs_1_ = bf16[80,3584]{1,0:T(8,128)(2,1)S(1)} collective-permute-done((bf16[80,3584]{1,0:T(8,128)(2,1)}, bf16[80,3584]{1,0:T(8,128)(2,1)S(1)}, u32[]{:S(2)}, u32[]{:S(2)}) %collective-permute-start.1) | collective-permute-done | bytes 573472 | tf_op jit(solution)/shard_map/chip_0/ppermute | solution.py:40
  20.4 0.8 copy-done.10
  21.3 0.0 collective-permute-start.2
  21.3 10.6 %collective-permute-done.7.refs_0_ = bf16[80,3584]{1,0:T(8,128)(2,1)} collective-permute-done((bf16[80,3584]{1,0:T(8,128)(2,1)}, bf16[80,3584]{1,0:T(8,128)(2,1)}, u32[]{:S(2)}, u32[]{:S(2)}) %collective-permute-start.7) | collective-permute-done | bytes 573472 | tf_op jit(solution)/shard_map/plane_3/ppermute | solution.py:40
  31.9 0.0 collective-permute-start.3
  31.9 0.0 collective-permute-done.2.refs_4_.refs_6_
  31.9 0.5 collective-permute-start.8
  32.4 1.9 %collective-permute-done.3.refs_5_.refs_7_ = bf16[16,80,256]{2,1,0:T(8,128)(2,1)} collective-permute-done((bf16[16,80,256]{2,1,0:T(8,128)(2,1)}, bf16[16,80,256]{2,1,0:T(8,128)(2,1)}, u32[]{:S(2)}, u32[]{:S(2)}) %collective-permute-start.3) | collective-permute-done | bytes 655392 | tf_op jit(solution)/shard_map/ppermute | solution.py:40
  34.3 2.6 %collective-permute-start.21 = (bf16[80,3584]{1,0:T(8,128)(2,1)}, bf16[80,3584]{1,0:T(8,128)(2,1)S(1)}, u32[]{:S(2)}, u32[]{:S(2)}) collective-permute-start(bf16[80,3584]{1,0:T(8,128)(2,1)} %get-tuple-element.46), channel_id=1, source_target_pairs={{0,12},{1,13},{2,14},{3,15},{4,8},{5,9},{6,10},{7,11},{8,4},{9,5},... | collective-permute-start | bytes 1720328 | tf_op jit(solution)/shard_map/plane_4/ppermute | solution.py:40
  36.9 0.0 collective-permute-done.4.refs_9_.refs_11_
  36.9 0.0 collective-permute-done.5.refs_10_.refs_12_
  36.9 0.0 collective-permute-done.6.refs_11_.refs_13_
  37.0 0.0 copy-start
  37.0 1.5 copy-done
  38.5 1.5 copy-done.2
  40.0 1.5 copy-done.4
  41.5 1.1 copy-done.7
  42.6 1.1 copy-done.9
  43.6 1.1 copy-done.11
  44.7 6.5 %pieces.4 = (bf16[80,3584]{1,0:T(8,128)(2,1)S(1)}, bf16[80,3584]{1,0:T(8,128)(2,1)S(1)}) custom-call(s32[2]{0:T(128)S(1)} %broadcast_add_fusion.3.source_ref, bf16[80,3584]{1,0:T(8,128)(2,1)S(1)} %copy-done.9, bf16[80,3584]{1,0:T(8,128)(2,1)S(1)} %copy-done.11, bf16[16,80,256]{2,1,0:T(8,128)(2,1)S(1)} %bitcast.34, bf16[16,80,256]{2,1,0:T(8,128)(2,1)S(1)} %bitcast.39, ...), custom_call_target="tpu_custom_call" | custom-call | flops 1000 | bytes 1000 | tf_op jit(solution)/shard_map/pieces_0/pieces/pallas_call | solution.py:228
  51.2 0.0 collective-permute-done.8.refs_1_
  51.2 0.0 copy-start.12
  51.2 0.6 collective-permute-start.9
  51.8 7.2 %pieces.6 = (bf16[80,3584]{1,0:T(8,128)(2,1)S(1)}, bf16[80,3584]{1,0:T(8,128)(2,1)S(1)}) custom-call(s32[2]{0:T(128)S(1)} %broadcast_add_fusion.1.source_ref, bf16[80,3584]{1,0:T(8,128)(2,1)} %collective-permute-done.7.refs_0_, bf16[80,3584]{1,0:T(8,128)(2,1)} %collective-permute-done.8.refs_1_, bf16[16,80,256]{2,1,0:T(8,128)(2,1)S(1)} %bitcast.35, ...), custom_call_target="tpu_custom_call" | custom-call | flops 99999997952 | bytes 1000 | tf_op jit(solution)/shard_map/pieces_2/pieces/pallas_call | solution.py:228
  59.1 1.6 %collective-permute-start.15 = (bf16[80,3584]{1,0:T(8,128)(2,1)S(1)}, bf16[80,3584]{1,0:T(8,128)(2,1)S(1)}, u32[]{:S(2)}, u32[]{:S(2)}) collective-permute-start(bf16[80,3584]{1,0:T(8,128)(2,1)S(1)} %get-tuple-element.40), channel_id=1, source_target_pairs={{0,2},{1,3},{2,0},{3,1},{4,6},{5,7},{6,4},{7,5},{8,10},{9,11},{10,... | collective-permute-start | bytes 1720328 | tf_op jit(solution)/shard_map/chip_back_3/ppermute | solution.py:40
  60.7 2.2 %collective-permute-start.11 = (bf16[48,3584]{1,0:T(8,128)(2,1)S(1)}, bf16[48,3584]{1,0:T(8,128)(2,1)S(1)}, u32[]{:S(2)}, u32[]{:S(2)}) collective-permute-start(bf16[48,3584]{1,0:T(8,128)(2,1)S(1)} %copy-done.13), channel_id=1, source_target_pairs={{0,4},{1,5},{2,6},{3,7},{4,0},{5,1},{6,2},{7,3},{8,12},{9,13},{10,... | collective-permute-start | bytes 1032200 | tf_op jit(solution)/shard_map/plane_1/ppermute | solution.py:40
  62.9 1.5 %collective-permute-start = (s32[2,128]{1,0:T(2,128)S(1)}, s32[2,128]{1,0:T(2,128)S(1)}, u32[]{:S(2)}, u32[]{:S(2)}) collective-permute-start(s32[2,128]{1,0:T(2,128)S(1)} %bitcast.46), channel_id=1, source_target_pairs={{0,16},{1,17},{2,18},{3,19},{4,20},{5,21},{6,22},{7,23},{8,24},{9,... | collective-permute-start | bytes 3080 | tf_op jit(solution)/shard_map/ppermute | solution.py:50
  64.4 2.0 %collective-permute-done.ids_ref = s32[2,128]{1,0:T(2,128)S(1)} collective-permute-done((s32[2,128]{1,0:T(2,128)S(1)}, s32[2,128]{1,0:T(2,128)S(1)}, u32[]{:S(2)}, u32[]{:S(2)}) %collective-permute-start) | collective-permute-done | bytes 1056 | tf_op jit(solution)/shard_map/ppermute | solution.py:50
  66.5 0.1 collective-permute-start.12
  66.6 8.8 %collective-permute-done.12.refs_1_ = bf16[32,3584]{1,0:T(8,128)(2,1)S(1)} collective-permute-done((bf16[32,3584]{1,0:T(8,128)(2,1)S(1)}, bf16[32,3584]{1,0:T(8,128)(2,1)S(1)}, u32[]{:S(2)}, u32[]{:S(2)}) %collective-permute-start.12) | collective-permute-done | bytes 229408 | tf_op jit(solution)/shard_map/plane_2/ppermute | solution.py:40
  75.3 0.5 collective-permute-start.14
  75.8 0.0 collective-permute-done.21.refs_0_
  75.8 1.5 %collective-permute-start.22 = (bf16[80,3584]{1,0:T(8,128)(2,1)S(1)}, bf16[80,3584]{1,0:T(8,128)(2,1)S(1)}, u32[]{:S(2)}, u32[]{:S(2)}) collective-permute-start(bf16[80,3584]{1,0:T(8,128)(2,1)S(1)} %collective-permute-done.21.refs_0_), channel_id=1, source_target_pairs={{0,2},{1,3},{2,0},{3,1},{4,6},{5,7},{6,4},{7,5},{8,10},{9,11},{10,... | collective-permute-start | bytes 1720328 | tf_op jit(solution)/shard_map/chip_4/ppermute | solution.py:40
  77.4 0.0 collective-permute-done.11.refs_0_
  77.4 0.0 collective-permute-done.9
  77.4 0.5 collective-permute-start.13
  77.9 1.6 %collective-permute-done.15 = bf16[80,3584]{1,0:T(8,128)(2,1)S(1)} collective-permute-done((bf16[80,3584]{1,0:T(8,128)(2,1)S(1)}, bf16[80,3584]{1,0:T(8,128)(2,1)S(1)}, u32[]{:S(2)}, u32[]{:S(2)}) %collective-permute-start.15) | collective-permute-done | bytes 573472 | tf_op jit(solution)/shard_map/chip_back_3/ppermute | solution.py:40
  79.4 0.1 add_convert_fusion.1
  79.6 5.3 %collective-permute-start.16 = (bf16[80,3584]{1,0:T(8,128)(2,1)S(1)}, bf16[80,3584]{1,0:T(8,128)(2,1)S(1)}, u32[]{:S(2)}, u32[]{:S(2)}) collective-permute-start(bf16[80,3584]{1,0:T(8,128)(2,1)S(1)} %add_convert_fusion.1), channel_id=1, source_target_pairs={{0,24},{1,25},{2,26},{3,27},{4,28},{5,29},{6,30},{7,31},{8,16},{9,... | collective-permute-start | bytes 1720328 | tf_op jit(solution)/shard_map/plane_back_3/ppermute | solution.py:50
  84.9 11.8 %collective-permute-done.22.refs_1_ = bf16[80,3584]{1,0:T(8,128)(2,1)S(1)} collective-permute-done((bf16[80,3584]{1,0:T(8,128)(2,1)S(1)}, bf16[80,3584]{1,0:T(8,128)(2,1)S(1)}, u32[]{:S(2)}, u32[]{:S(2)}) %collective-permute-start.22) | collective-permute-done | bytes 573472 | tf_op jit(solution)/shard_map/chip_4/ppermute | solution.py:40
  96.7 6.3 %pieces.7 = (bf16[80,3584]{1,0:T(8,128)(2,1)S(1)}, bf16[80,3584]{1,0:T(8,128)(2,1)S(1)}) custom-call(s32[2]{0:T(128)S(1)} %broadcast_add_fusion.source_ref, bf16[80,3584]{1,0:T(8,128)(2,1)S(1)} %collective-permute-done.21.refs_0_, bf16[80,3584]{1,0:T(8,128)(2,1)S(1)} %collective-permute-done.22.refs_1_, bf16[16,80,256]{2,1,0:T(8,128)(2,1)S(1)} %bitcast.36, ...), custom_call_target="tpu_custom_call" | custom-call | flops 99999997952 | bytes 1000 | tf_op jit(solution)/shard_map/pieces_3/pieces/pallas_call | solution.py:228
  103.0 0.6 collective-permute-start.23
  103.6 0.1 add_convert_fusion.2
  103.7 1.6 %collective-permute-start.10 = (bf16[80,3584]{1,0:T(8,128)(2,1)S(1)}, bf16[80,3584]{1,0:T(8,128)(2,1)S(1)}, u32[]{:S(2)}, u32[]{:S(2)}) collective-permute-start(bf16[80,3584]{1,0:T(8,128)(2,1)S(1)} %add_convert_fusion.2), channel_id=1, source_target_pairs={{0,16},{1,17},{2,18},{3,19},{4,20},{5,21},{6,22},{7,23},{8,24},{9,... | collective-permute-start | bytes 1720328 | tf_op jit(solution)/shard_map/plane_back_0/ppermute | solution.py:50
  105.3 0.0 collective-permute-done.14.refs_3_
  105.3 6.9 %pieces.5 = (bf16[48,3584]{1,0:T(8,128)(2,1)S(1)}, bf16[32,3584]{1,0:T(8,128)(2,1)S(1)}, bf16[48,3584]{1,0:T(8,128)(2,1)S(1)}, bf16[32,3584]{1,0:T(8,128)(2,1)S(1)}) custom-call(s32[2]{0:T(128)S(1)} %broadcast_add_fusion.2.source_ref, bf16[48,3584]{1,0:T(8,128)(2,1)S(1)} %collective-permute-done.11.refs_0_, ...), custom_call_target="tpu_custom_call" | custom-call | flops 1000 | bytes 1000 | tf_op jit(solution)/shard_map/pieces_1/pieces/pallas_call | solution.py:228
  112.3 1.5 %collective-permute-start.17 = (bf16[48,3584]{1,0:T(8,128)(2,1)S(1)}, bf16[48,3584]{1,0:T(8,128)(2,1)S(1)}, u32[]{:S(2)}, u32[]{:S(2)}) collective-permute-start(bf16[48,3584]{1,0:T(8,128)(2,1)S(1)} %get-tuple-element.41), channel_id=1, source_target_pairs={{0,2},{1,3},{2,0},{3,1},{4,6},{5,7},{6,4},{7,5},{8,10},{9,11},{10,... | collective-permute-start | bytes 1032200 | tf_op jit(solution)/shard_map/chip_back_1/ppermute | solution.py:40
  113.8 0.6 collective-permute-start.19
  114.4 4.6 %collective-permute-done.23 = bf16[80,3584]{1,0:T(8,128)(2,1)S(1)} collective-permute-done((bf16[80,3584]{1,0:T(8,128)(2,1)S(1)}, bf16[80,3584]{1,0:T(8,128)(2,1)S(1)}, u32[]{:S(2)}, u32[]{:S(2)}) %collective-permute-start.23) | collective-permute-done | bytes 573472 | tf_op jit(solution)/shard_map/chip_back_4/ppermute | solution.py:40
  119.0 0.1 add_convert_fusion
  119.1 3.0 %collective-permute-start.24 = (bf16[80,3584]{1,0:T(8,128)(2,1)S(1)}, bf16[80,3584]{1,0:T(8,128)(2,1)S(1)}, u32[]{:S(2)}, u32[]{:S(2)}) collective-permute-start(bf16[80,3584]{1,0:T(8,128)(2,1)S(1)} %add_convert_fusion), channel_id=1, source_target_pairs={{0,28},{1,29},{2,30},{3,31},{4,24},{5,25},{6,26},{7,27},{8,20},{9,... | collective-permute-start | bytes 1720328 | tf_op jit(solution)/shard_map/plane_back_4/ppermute | solution.py:50
  122.1 3.5 %collective-permute-done.17 = bf16[48,3584]{1,0:T(8,128)(2,1)S(1)} collective-permute-done((bf16[48,3584]{1,0:T(8,128)(2,1)S(1)}, bf16[48,3584]{1,0:T(8,128)(2,1)S(1)}, u32[]{:S(2)}, u32[]{:S(2)}) %collective-permute-start.17) | collective-permute-done | bytes 344096 | tf_op jit(solution)/shard_map/chip_back_1/ppermute | solution.py:40
  125.6 0.1 add_convert_fusion.3
  125.7 3.3 %collective-permute-start.18 = (bf16[48,3584]{1,0:T(8,128)(2,1)S(1)}, bf16[48,3584]{1,0:T(8,128)(2,1)S(1)}, u32[]{:S(2)}, u32[]{:S(2)}) collective-permute-start(bf16[48,3584]{1,0:T(8,128)(2,1)S(1)} %add_convert_fusion.3), channel_id=1, source_target_pairs={{0,20},{1,21},{2,22},{3,23},{4,16},{5,17},{6,18},{7,19},{8,28},{9,... | collective-permute-start | bytes 1032200 | tf_op jit(solution)/shard_map/plane_back_1/ppermute | solution.py:50
  129.0 0.1 add_convert_fusion.4
  129.0 2.4 %collective-permute-start.20 = (bf16[32,3584]{1,0:T(8,128)(2,1)S(1)}, bf16[32,3584]{1,0:T(8,128)(2,1)S(1)}, u32[]{:S(2)}, u32[]{:S(2)}) collective-permute-start(bf16[32,3584]{1,0:T(8,128)(2,1)S(1)} %add_convert_fusion.4), channel_id=1, source_target_pairs={{0,20},{1,21},{2,22},{3,23},{4,16},{5,17},{6,18},{7,19},{8,28},{9,... | collective-permute-start | bytes 688136 | tf_op jit(solution)/shard_map/plane_back_2/ppermute | solution.py:50
  131.4 15.7 %collective-permute-done.20.refs_2_ = bf16[32,3584]{1,0:T(8,128)(2,1)S(1)} collective-permute-done((bf16[32,3584]{1,0:T(8,128)(2,1)S(1)}, bf16[32,3584]{1,0:T(8,128)(2,1)S(1)}, u32[]{:S(2)}, u32[]{:S(2)}) %collective-permute-start.20) | collective-permute-done | bytes 229408 | tf_op jit(solution)/shard_map/plane_back_2/ppermute | solution.py:50
  147.2 3.2 %combine.1 = bf16[128,3584]{1,0:T(8,128)(2,1)} custom-call(s32[1]{0:T(128)} %bitcast.own_ref, s32[2,128]{1,0:T(2,128)S(1)} %collective-permute-done.ids_ref, bf16[80,3584]{1,0:T(8,128)(2,1)S(1)} %collective-permute-done.10.refs_0_, bf16[48,3584]{1,0:T(8,128)(2,1)S(1)} %collective-permute-done.18.refs_1_, ...), custom_call_target="tpu_custom_call" | custom-call | flops 1000 | bytes 1000 | tf_op jit(solution)/shard_map/combine/pallas_call | solution.py:151
  (31 shorter events, 0.1 us)
Async XLA Ops:
  0.0 37.0 %copy-start.6 = (bf16[1,1,16,80,256]{4,3,2,1,0:T(8,128)(2,1)S(1)}, bf16[1,1,16,80,256]{4,3,2,1,0:T(8,128)(2,1)}, u32[]{:S(2)}) copy-start(bf16[1,1,16,80,256]{4,3,2,1,0:T(8,128)(2,1)} %param.15) | copy-start | bytes 1966084
  0.0 36.9 %collective-permute-start.4 = (bf16[3584,256]{1,0:T(8,128)(2,1)}, bf16[3584,256]{1,0:T(8,128)(2,1)S(1)}, u32[]{:S(2)}, u32[]{:S(2)}) collective-permute-start(bf16[3584,256]{1,0:T(8,128)(2,1)} %bitcast.18), channel_id=1, source_target_pairs={{0,1},{1,0},{2,3},{3,2},{4,5},{5,4},{6,7},{7,6},{8,9},{9,8},{10,11... | collective-permute-start | bytes 5505032 | tf_op jit(solution)/shard_map/ppermute | solution.py:40
  0.0 36.9 %collective-permute-start.5 = (bf16[3584,256]{1,0:T(8,128)(2,1)}, bf16[3584,256]{1,0:T(8,128)(2,1)}, u32[]{:S(2)}, u32[]{:S(2)}) collective-permute-start(bf16[3584,256]{1,0:T(8,128)(2,1)} %bitcast.23), channel_id=1, source_target_pairs={{0,1},{1,0},{2,3},{3,2},{4,5},{5,4},{6,7},{7,6},{8,9},{9,8},{10,11... | collective-permute-start | bytes 5505032 | tf_op jit(solution)/shard_map/ppermute | solution.py:40
  0.5 36.4 %collective-permute-start.6 = (bf16[256,3584]{1,0:T(8,128)(2,1)}, bf16[256,3584]{1,0:T(8,128)(2,1)}, u32[]{:S(2)}, u32[]{:S(2)}) collective-permute-start(bf16[256,3584]{1,0:T(8,128)(2,1)} %bitcast.28), channel_id=1, source_target_pairs={{0,1},{1,0},{2,3},{3,2},{4,5},{5,4},{6,7},{7,6},{8,9},{9,8},{10,11... | collective-permute-start | bytes 5505032 | tf_op jit(solution)/shard_map/ppermute | solution.py:40
  4.9 15.5 %collective-permute-start.1 = (bf16[80,3584]{1,0:T(8,128)(2,1)}, bf16[80,3584]{1,0:T(8,128)(2,1)S(1)}, u32[]{:S(2)}, u32[]{:S(2)}) collective-permute-start(bf16[80,3584]{1,0:T(8,128)(2,1)} %get-tuple-element.28.refs_0_), channel_id=1, source_target_pairs={{0,2},{1,3},{2,0},{3,1},{4,6},{5,7},{6,4},{7,5},{8,10},{9,11},{10,... | collective-permute-start | bytes 1720328 | tf_op jit(solution)/shard_map/chip_0/ppermute | solution.py:40
  6.4 25.5 %collective-permute-start.7 = (bf16[80,3584]{1,0:T(8,128)(2,1)}, bf16[80,3584]{1,0:T(8,128)(2,1)}, u32[]{:S(2)}, u32[]{:S(2)}) collective-permute-start(bf16[80,3584]{1,0:T(8,128)(2,1)} %get-tuple-element.31), channel_id=1, source_target_pairs={{0,8},{1,9},{2,10},{3,11},{4,12},{5,13},{6,14},{7,15},{8,0},{9,1},... | collective-permute-start | bytes 1720328 | tf_op jit(solution)/shard_map/plane_3/ppermute | solution.py:40
  20.4 0.8 copy-start.10
  21.3 10.6 %collective-permute-start.2 = (bf16[16,80,256]{2,1,0:T(8,128)(2,1)}, bf16[16,80,256]{2,1,0:T(8,128)(2,1)S(1)}, u32[]{:S(2)}, u32[]{:S(2)}) collective-permute-start(bf16[16,80,256]{2,1,0:T(8,128)(2,1)} %bitcast.33), channel_id=1, source_target_pairs={{0,1},{1,0},{2,3},{3,2},{4,5},{5,4},{6,7},{7,6},{8,9},{9,8},{10,11... | collective-permute-start | bytes 1966088 | tf_op jit(solution)/shard_map/ppermute | solution.py:40
  31.9 2.4 %collective-permute-start.3 = (bf16[16,80,256]{2,1,0:T(8,128)(2,1)}, bf16[16,80,256]{2,1,0:T(8,128)(2,1)}, u32[]{:S(2)}, u32[]{:S(2)}) collective-permute-start(bf16[16,80,256]{2,1,0:T(8,128)(2,1)} %bitcast.38), channel_id=1, source_target_pairs={{0,1},{1,0},{2,3},{3,2},{4,5},{5,4},{6,7},{7,6},{8,9},{9,8},{10,11... | collective-permute-start | bytes 1966088 | tf_op jit(solution)/shard_map/ppermute | solution.py:40
  31.9 19.3 %collective-permute-start.8 = (bf16[80,3584]{1,0:T(8,128)(2,1)}, bf16[80,3584]{1,0:T(8,128)(2,1)}, u32[]{:S(2)}, u32[]{:S(2)}) collective-permute-start(bf16[80,3584]{1,0:T(8,128)(2,1)} %collective-permute-done.7.refs_0_), channel_id=1, source_target_pairs={{0,2},{1,3},{2,0},{3,1},{4,6},{5,7},{6,4},{7,5},{8,10},{9,11},{10,... | collective-permute-start | bytes 1720328 | tf_op jit(solution)/shard_map/chip_3/ppermute | solution.py:40
  34.3 41.5 %collective-permute-start.21 = (bf16[80,3584]{1,0:T(8,128)(2,1)}, bf16[80,3584]{1,0:T(8,128)(2,1)S(1)}, u32[]{:S(2)}, u32[]{:S(2)}) collective-permute-start(bf16[80,3584]{1,0:T(8,128)(2,1)} %get-tuple-element.46), channel_id=1, source_target_pairs={{0,12},{1,13},{2,14},{3,15},{4,8},{5,9},{6,10},{7,11},{8,4},{9,5},... | collective-permute-start | bytes 1720328 | tf_op jit(solution)/shard_map/plane_4/ppermute | solution.py:40
  37.0 1.5 copy-start
  38.5 1.5 copy-start.2
  40.0 1.5 copy-start.4
  41.5 1.1 copy-start.7
  42.6 1.1 copy-start.9
  43.6 1.1 copy-start.11
  44.7 7.2 %copy-start.1 = (bf16[1,1,3584,256]{3,2,1,0:T(8,128)(2,1)S(1)}, bf16[1,1,3584,256]{3,2,1,0:T(8,128)(2,1)}, u32[]{:S(2)}) copy-start(bf16[1,1,3584,256]{3,2,1,0:T(8,128)(2,1)} %param.17) | copy-start | bytes 5505028
  44.7 7.2 %copy-start.3 = (bf16[1,1,3584,256]{3,2,1,0:T(8,128)(2,1)S(1)}, bf16[1,1,3584,256]{3,2,1,0:T(8,128)(2,1)}, u32[]{:S(2)}) copy-start(bf16[1,1,3584,256]{3,2,1,0:T(8,128)(2,1)} %param.18) | copy-start | bytes 5505028
  44.7 7.2 %copy-start.5 = (bf16[1,1,256,3584]{3,2,1,0:T(8,128)(2,1)S(1)}, bf16[1,1,256,3584]{3,2,1,0:T(8,128)(2,1)}, u32[]{:S(2)}) copy-start(bf16[1,1,256,3584]{3,2,1,0:T(8,128)(2,1)} %param.19) | copy-start | bytes 5505028
  44.7 7.2 %copy-start.8 = (bf16[1,1,16,80,256]{4,3,2,1,0:T(8,128)(2,1)S(1)}, bf16[1,1,16,80,256]{4,3,2,1,0:T(8,128)(2,1)}, u32[]{:S(2)}) copy-start(bf16[1,1,16,80,256]{4,3,2,1,0:T(8,128)(2,1)} %param.16) | copy-start | bytes 1966084
  51.2 9.5 %copy-start.13 = (bf16[48,3584]{1,0:T(8,128)(2,1)S(1)}, bf16[48,3584]{1,0:T(8,128)(2,1)}, u32[]{:S(2)}) copy-start(bf16[48,3584]{1,0:T(8,128)(2,1)} %get-tuple-element.34) | copy-start | bytes 1032196
  51.2 11.7 %copy-start.12 = (s32[1,128,2]{1,2,0:T(2,128)S(1)}, s32[1,128,2]{1,2,0:T(2,128)}, u32[]{:S(2)}) copy-start(s32[1,128,2]{1,2,0:T(2,128)} %param.13) | copy-start | bytes 3076
  51.2 15.3 %copy-start.14 = (bf16[32,3584]{1,0:T(8,128)(2,1)S(1)}, bf16[32,3584]{1,0:T(8,128)(2,1)}, u32[]{:S(2)}) copy-start(bf16[32,3584]{1,0:T(8,128)(2,1)} %get-tuple-element.35) | copy-start | bytes 688132
  51.2 26.1 %collective-permute-start.9 = (bf16[80,3584]{1,0:T(8,128)(2,1)S(1)}, bf16[80,3584]{1,0:T(8,128)(2,1)S(1)}, u32[]{:S(2)}, u32[]{:S(2)}) collective-permute-start(bf16[80,3584]{1,0:T(8,128)(2,1)S(1)} %get-tuple-element.32), channel_id=1, source_target_pairs={{0,2},{1,3},{2,0},{3,1},{4,6},{5,7},{6,4},{7,5},{8,10},{9,11},{10,... | collective-permute-start | bytes 1720328 | tf_op jit(solution)/shard_map/chip_back_0/ppermute | solution.py:40
  59.1 20.4 %collective-permute-start.15 = (bf16[80,3584]{1,0:T(8,128)(2,1)S(1)}, bf16[80,3584]{1,0:T(8,128)(2,1)S(1)}, u32[]{:S(2)}, u32[]{:S(2)}) collective-permute-start(bf16[80,3584]{1,0:T(8,128)(2,1)S(1)} %get-tuple-element.40), channel_id=1, source_target_pairs={{0,2},{1,3},{2,0},{3,1},{4,6},{5,7},{6,4},{7,5},{8,10},{9,11},{10,... | collective-permute-start | bytes 1720328 | tf_op jit(solution)/shard_map/chip_back_3/ppermute | solution.py:40
  60.7 16.7 %collective-permute-start.11 = (bf16[48,3584]{1,0:T(8,128)(2,1)S(1)}, bf16[48,3584]{1,0:T(8,128)(2,1)S(1)}, u32[]{:S(2)}, u32[]{:S(2)}) collective-permute-start(bf16[48,3584]{1,0:T(8,128)(2,1)S(1)} %copy-done.13), channel_id=1, source_target_pairs={{0,4},{1,5},{2,6},{3,7},{4,0},{5,1},{6,2},{7,3},{8,12},{9,13},{10,... | collective-permute-start | bytes 1032200 | tf_op jit(solution)/shard_map/plane_1/ppermute | solution.py:40
  62.9 3.6 %collective-permute-start = (s32[2,128]{1,0:T(2,128)S(1)}, s32[2,128]{1,0:T(2,128)S(1)}, u32[]{:S(2)}, u32[]{:S(2)}) collective-permute-start(s32[2,128]{1,0:T(2,128)S(1)} %bitcast.46), channel_id=1, source_target_pairs={{0,16},{1,17},{2,18},{3,19},{4,20},{5,21},{6,22},{7,23},{8,24},{9,... | collective-permute-start | bytes 3080 | tf_op jit(solution)/shard_map/ppermute | solution.py:50
  66.5 8.9 %collective-permute-start.12 = (bf16[32,3584]{1,0:T(8,128)(2,1)S(1)}, bf16[32,3584]{1,0:T(8,128)(2,1)S(1)}, u32[]{:S(2)}, u32[]{:S(2)}) collective-permute-start(bf16[32,3584]{1,0:T(8,128)(2,1)S(1)} %copy-done.14), channel_id=1, source_target_pairs={{0,4},{1,5},{2,6},{3,7},{4,0},{5,1},{6,2},{7,3},{8,12},{9,13},{10,... | collective-permute-start | bytes 688136 | tf_op jit(solution)/shard_map/plane_2/ppermute | solution.py:40
  75.3 30.0 %collective-permute-start.14 = (bf16[32,3584]{1,0:T(8,128)(2,1)S(1)}, bf16[32,3584]{1,0:T(8,128)(2,1)S(1)}, u32[]{:S(2)}, u32[]{:S(2)}) collective-permute-start(bf16[32,3584]{1,0:T(8,128)(2,1)S(1)} %collective-permute-done.12.refs_1_), channel_id=1, source_target_pairs={{0,2},{1,3},{2,0},{3,1},{4,6},{5,7},{6,4},{7,5},{8,10},{9,11},{10,... | collective-permute-start | bytes 688136 | tf_op jit(solution)/shard_map/chip_2/ppermute | solution.py:40
  75.8 20.8 %collective-permute-start.22 = (bf16[80,3584]{1,0:T(8,128)(2,1)S(1)}, bf16[80,3584]{1,0:T(8,128)(2,1)S(1)}, u32[]{:S(2)}, u32[]{:S(2)}) collective-permute-start(bf16[80,3584]{1,0:T(8,128)(2,1)S(1)} %collective-permute-done.21.refs_0_), channel_id=1, source_target_pairs={{0,2},{1,3},{2,0},{3,1},{4,6},{5,7},{6,4},{7,5},{8,10},{9,11},{10,... | collective-permute-start | bytes 1720328 | tf_op jit(solution)/shard_map/chip_4/ppermute | solution.py:40
  77.4 27.9 %collective-permute-start.13 = (bf16[48,3584]{1,0:T(8,128)(2,1)S(1)}, bf16[48,3584]{1,0:T(8,128)(2,1)S(1)}, u32[]{:S(2)}, u32[]{:S(2)}) collective-permute-start(bf16[48,3584]{1,0:T(8,128)(2,1)S(1)} %collective-permute-done.11.refs_0_), channel_id=1, source_target_pairs={{0,2},{1,3},{2,0},{3,1},{4,6},{5,7},{6,4},{7,5},{8,10},{9,11},{10,... | collective-permute-start | bytes 1032200 | tf_op jit(solution)/shard_map/chip_1/ppermute | solution.py:40
  79.6 32.7 %collective-permute-start.16 = (bf16[80,3584]{1,0:T(8,128)(2,1)S(1)}, bf16[80,3584]{1,0:T(8,128)(2,1)S(1)}, u32[]{:S(2)}, u32[]{:S(2)}) collective-permute-start(bf16[80,3584]{1,0:T(8,128)(2,1)S(1)} %add_convert_fusion.1), channel_id=1, source_target_pairs={{0,24},{1,25},{2,26},{3,27},{4,28},{5,29},{6,30},{7,31},{8,16},{9,... | collective-permute-start | bytes 1720328 | tf_op jit(solution)/shard_map/plane_back_3/ppermute | solution.py:50
  103.0 16.0 %collective-permute-start.23 = (bf16[80,3584]{1,0:T(8,128)(2,1)S(1)}, bf16[80,3584]{1,0:T(8,128)(2,1)S(1)}, u32[]{:S(2)}, u32[]{:S(2)}) collective-permute-start(bf16[80,3584]{1,0:T(8,128)(2,1)S(1)} %get-tuple-element.50), channel_id=1, source_target_pairs={{0,2},{1,3},{2,0},{3,1},{4,6},{5,7},{6,4},{7,5},{8,10},{9,11},{10,... | collective-permute-start | bytes 1720328 | tf_op jit(solution)/shard_map/chip_back_4/ppermute | solution.py:40
  103.7 27.7 %collective-permute-start.10 = (bf16[80,3584]{1,0:T(8,128)(2,1)S(1)}, bf16[80,3584]{1,0:T(8,128)(2,1)S(1)}, u32[]{:S(2)}, u32[]{:S(2)}) collective-permute-start(bf16[80,3584]{1,0:T(8,128)(2,1)S(1)} %add_convert_fusion.2), channel_id=1, source_target_pairs={{0,16},{1,17},{2,18},{3,19},{4,20},{5,21},{6,22},{7,23},{8,24},{9,... | collective-permute-start | bytes 1720328 | tf_op jit(solution)/shard_map/plane_back_0/ppermute | solution.py:50
  112.3 13.3 %collective-permute-start.17 = (bf16[48,3584]{1,0:T(8,128)(2,1)S(1)}, bf16[48,3584]{1,0:T(8,128)(2,1)S(1)}, u32[]{:S(2)}, u32[]{:S(2)}) collective-permute-start(bf16[48,3584]{1,0:T(8,128)(2,1)S(1)} %get-tuple-element.41), channel_id=1, source_target_pairs={{0,2},{1,3},{2,0},{3,1},{4,6},{5,7},{6,4},{7,5},{8,10},{9,11},{10,... | collective-permute-start | bytes 1032200 | tf_op jit(solution)/shard_map/chip_back_1/ppermute | solution.py:40
  113.8 15.2 %collective-permute-start.19 = (bf16[32,3584]{1,0:T(8,128)(2,1)S(1)}, bf16[32,3584]{1,0:T(8,128)(2,1)S(1)}, u32[]{:S(2)}, u32[]{:S(2)}) collective-permute-start(bf16[32,3584]{1,0:T(8,128)(2,1)S(1)} %get-tuple-element.44), channel_id=1, source_target_pairs={{0,2},{1,3},{2,0},{3,1},{4,6},{5,7},{6,4},{7,5},{8,10},{9,11},{10,... | collective-permute-start | bytes 688136 | tf_op jit(solution)/shard_map/chip_back_2/ppermute | solution.py:40
  119.1 28.0 %collective-permute-start.24 = (bf16[80,3584]{1,0:T(8,128)(2,1)S(1)}, bf16[80,3584]{1,0:T(8,128)(2,1)S(1)}, u32[]{:S(2)}, u32[]{:S(2)}) collective-permute-start(bf16[80,3584]{1,0:T(8,128)(2,1)S(1)} %add_convert_fusion), channel_id=1, source_target_pairs={{0,28},{1,29},{2,30},{3,31},{4,24},{5,25},{6,26},{7,27},{8,20},{9,... | collective-permute-start | bytes 1720328 | tf_op jit(solution)/shard_map/plane_back_4/ppermute | solution.py:50
  125.7 21.5 %collective-permute-start.18 = (bf16[48,3584]{1,0:T(8,128)(2,1)S(1)}, bf16[48,3584]{1,0:T(8,128)(2,1)S(1)}, u32[]{:S(2)}, u32[]{:S(2)}) collective-permute-start(bf16[48,3584]{1,0:T(8,128)(2,1)S(1)} %add_convert_fusion.3), channel_id=1, source_target_pairs={{0,20},{1,21},{2,22},{3,23},{4,16},{5,17},{6,18},{7,19},{8,28},{9,... | collective-permute-start | bytes 1032200 | tf_op jit(solution)/shard_map/plane_back_1/ppermute | solution.py:50
  129.0 18.1 %collective-permute-start.20 = (bf16[32,3584]{1,0:T(8,128)(2,1)S(1)}, bf16[32,3584]{1,0:T(8,128)(2,1)S(1)}, u32[]{:S(2)}, u32[]{:S(2)}) collective-permute-start(bf16[32,3584]{1,0:T(8,128)(2,1)S(1)} %add_convert_fusion.4), channel_id=1, source_target_pairs={{0,20},{1,21},{2,22},{3,23},{4,16},{5,17},{6,18},{7,19},{8,28},{9,... | collective-permute-start | bytes 688136 | tf_op jit(solution)/shard_map/plane_back_2/ppermute | solution.py:50
